TPU v7x, 32 devices: a whole 2x2x4 slice. The times are simulated.
32 devices in a mesh: rows: 4 (over y, x), cols: 8 (over z, core).
Axes of the slice: x: 2, y: 2, z: 4, core: 2. Of those that a mesh axis runs over, the one named last changes fastest.
Arguments:
- coefficients: float32 [1024, 2048], P('cols', 'rows'), may hold values from -6 to 6
- factor_panel: float32 [2048, 1024], P('rows'), may hold values from -0.125 to 0.125
- block_inverse: float32 [2048, 512], P('rows'), may hold values from -0.044194174 to 2, as said below
- train_inputs: float32 [14, 2048], P(None, 'rows'), may hold values from 0 to 1
- query_points: float32 [14, 8192], replicated, may hold values from 0 to 1
- inv_length: float32 [14], replicated, may hold values from 0.25 to 2
- amplitude: float32 [1024], P('cols'), may hold values from 0.02 to 0.2
Outputs:
- weights: float32 [1024, 2048], P('cols', 'rows')
- predicted_mean: float32 [1024, 8192], P('cols', 'rows')
Inputs may be any that keep to these rules, and one draw needn't show every extreme that they name: `block_inverse`: each block of 512 rows is lower triangular, with diagonal entries from 1 to 2.
All inputs are finite; a program needn't handle non-finite values.
Results may differ from a plain program's by a relative error of at most 0.004.
Values may be sent and summed in bfloat16 or wider, within the bound.
A program may use at most 64 MiB of HBM per device.

v0:
```python
import jax
import jax.numpy as jnp
from jax import lax
from jax.sharding import PartitionSpec as P


def kernel_values(train_part, query_part, inv_length):
    squared = jnp.zeros((train_part.shape[1], query_part.shape[1]), jnp.float32)
    for dim_index in range(train_part.shape[0]):
        offset = (train_part[dim_index][:, None] - query_part[dim_index][None, :]) * inv_length[
            dim_index
        ]
        squared = squared + offset * offset
    return jnp.exp(-jnp.sqrt(squared + 1e-06)).astype(jnp.bfloat16)


def solve_product(left, right):
    return jnp.dot(left, right, precision=lax.Precision.HIGHEST, preferred_element_type=jnp.float32)


def on_device(
    coefficients, factor_panel, block_inverse, train_inputs, query_points, inv_length, amplitude
):
    block_len = coefficients.shape[1]
    row_index = lax.axis_index("rows")
    row_count = lax.axis_size("rows")
    solved_block = row_index >= 2
    factor_zero = factor_panel[:, :block_len]
    factor_one = factor_panel[:, block_len:]
    local_one = jnp.where(solved_block, solve_product(coefficients, factor_one), 0.0)
    local_zero = jnp.where(solved_block, solve_product(coefficients, factor_zero), 0.0)
    rest_one = lax.psum(local_one, "rows")
    weights_one = solve_product(coefficients - rest_one, block_inverse)
    carried = jnp.where(row_index == 1, solve_product(weights_one, factor_zero), local_zero)
    rest_zero = lax.psum(carried, "rows")
    weights_zero = solve_product(coefficients - rest_zero, block_inverse)
    weights = jnp.where(
        row_index == 0, weights_zero, jnp.where(row_index == 1, weights_one, coefficients)
    )
    weights_low = weights.astype(jnp.bfloat16)
    piece_len = query_points.shape[1] // row_count

    def single_piece(piece_index):
        chosen = lax.dynamic_slice_in_dim(query_points, piece_index * piece_len, piece_len, 1)
        return jnp.dot(
            weights_low,
            kernel_values(train_inputs, chosen, inv_length),
            preferred_element_type=jnp.float32,
        )

    summed = lax.psum_scatter(
        lax.map(single_piece, jnp.arange(1 * lax.axis_size("rows"), dtype=jnp.int32)),
        "rows",
        scatter_dimension=0,
        tiled=True,
    )
    predicted_mean = summed[0] * amplitude[:, None]
    return (weights, predicted_mean)


def solution(mesh):
    return jax.shard_map(
        on_device,
        mesh=mesh,
        in_specs=(
            P("cols", "rows"),
            P("rows", None),
            P("rows", None),
            P(None, "rows"),
            P(),
            P(),
            P("cols"),
        ),
        out_specs=(P("cols", "rows"), P("cols", "rows")),
        check_vma=False,
    )
```

profile of v0, /device:TPU:0, one launch (start us, length us, event | category | flops | bytes accessed | tf_op | source)
XLA Modules:
  0.0 265.3 jit_solution(2027380409180564326)
XLA Ops:
  7.2 0.0 copy-start
  7.2 0.0 copy-start.1
  7.2 0.0 copy-start.2
  7.2 0.0 all-reduce.4.cloned.1.call-start
  7.3 2.9 %convolution_select_fusion.2 = f32[128,512]{1,0:T(8,128)} fusion(f32[128,512]{1,0:T(8,128)} %param.9, f32[512,1024]{1,0:T(8,128)} %param.10, pred[]{:T(512)S(6)} %ge.3), kind=kOutput, calls=%fused_computation.50 | convolution fusion | flops 402718720 | bytes 1572865 | tf_op jit(solution)/shard_map/dot_general | solution.py:18
  10.1 0.0 all-reduce.4.cloned.1.call-update
  10.2 0.0 all-reduce.6.cloned.1.call-start
  10.2 47.0 %all-reduce.4.cloned.1.call-done = f32[128,512]{1,0:T(8,128)} async-done(((f32[128,512]{1,0:T(8,128)}), f32[128,512]{1,0:T(8,128)}) %all-reduce.4.cloned.1.call-update) | async-done | bytes 262160 | tf_op jit(solution)/shard_map/psum | solution.py:32
  57.2 0.0 copy-done
  57.2 1.7 fusion.49
  59.0 0.0 copy-start.4
  59.0 0.7 copy-done.4
  59.7 0.7 fusion.46
  60.4 0.0 copy-done.2
  60.4 1.4 fusion.43
  61.8 0.0 all-reduce.6.cloned.1.call-update
  61.9 0.2 reduce-scatter.4.cloned.1.call-start
  62.1 42.8 %all-reduce.6.cloned.1.call-done = f32[128,512]{1,0:T(8,128)} async-done(((f32[128,512]{1,0:T(8,128)}), f32[128,512]{1,0:T(8,128)}) %all-reduce.6.cloned.1.call-update) | async-done | bytes 262160 | tf_op jit(solution)/shard_map/psum | solution.py:35
  104.9 2.4 fusion.53
  107.3 0.0 copy-done.5
  107.3 96.2 %while.10 = (s32[]{:T(128)}, f32[4,128,2048]{2,1,0:T(8,128)}, f32[14,512]{1,0:T(8,128)S(1)}, s32[4]{0:T(128)S(1)}, f32[14,8192]{1,0:T(8,128)}, /*index=5*/f32[14...) while((s32[]{:T(128)}, f32[4,128,2048]{2,1,0:T(8,128)}, ...), condition=%wide.region_3.4_spmd, body=%wide.region_2.3_spmd.sunk | while | flops 329252896 | bytes 5805195 | solution.py:52
  107.3 0.6 dynamic_slice.8
  108.6 1.7 constant_dynamic-slice_fusion.2
  110.3 0.7 fusion.64
  111.0 18.9 %convolution_bitcast_fusion.2 = f32[1,128,2048]{1,2,0:T(8,128)S(1)} fusion(bf16[128,512]{1,0:T(8,128)(2,1)S(1)} %get-tuple-element.279, f32[]{:T(128)} %bitcast.103, f32[2048]{0:T(1024)S(1)} %bitcast.159, f32[512]{0:T(512)S(1)} %bitcast.161, f32[]{:T(128)} %bitcast.107, f32[2048]{0:T(1024)S(1)} %bitcast.147, f32[512]{0:T(512)S(1)} %bitcast.162, ...), kind=kOutput, calls=%fused_computation.1.clone.1 | convolution fusion | flops 329252864 | bytes 1323064 | tf_op jit(solution)/shard_map/while/body/eval_jaxpr/dot_general | solution.py:45
  129.9 0.3 copy.14
  130.3 1.1 constant_dynamic-update-slice_fusion.2
  131.3 0.6 dynamic_slice.8
  132.5 1.7 constant_dynamic-slice_fusion.2
  134.3 0.7 fusion.64
  135.0 18.9 %convolution_bitcast_fusion.2 = f32[1,128,2048]{1,2,0:T(8,128)S(1)} fusion(bf16[128,512]{1,0:T(8,128)(2,1)S(1)} %get-tuple-element.279, f32[]{:T(128)} %bitcast.103, f32[2048]{0:T(1024)S(1)} %bitcast.159, f32[512]{0:T(512)S(1)} %bitcast.161, f32[]{:T(128)} %bitcast.107, f32[2048]{0:T(1024)S(1)} %bitcast.147, f32[512]{0:T(512)S(1)} %bitcast.162, ...), kind=kOutput, calls=%fused_computation.1.clone.1 | convolution fusion | flops 329252864 | bytes 1323064 | tf_op jit(solution)/shard_map/while/body/eval_jaxpr/dot_general | solution.py:45
  153.9 0.3 copy.14
  154.2 1.1 constant_dynamic-update-slice_fusion.2
  155.3 0.6 dynamic_slice.8
  156.6 1.8 constant_dynamic-slice_fusion.2
  158.4 0.7 fusion.64
  159.1 18.9 %convolution_bitcast_fusion.2 = f32[1,128,2048]{1,2,0:T(8,128)S(1)} fusion(bf16[128,512]{1,0:T(8,128)(2,1)S(1)} %get-tuple-element.279, f32[]{:T(128)} %bitcast.103, f32[2048]{0:T(1024)S(1)} %bitcast.159, f32[512]{0:T(512)S(1)} %bitcast.161, f32[]{:T(128)} %bitcast.107, f32[2048]{0:T(1024)S(1)} %bitcast.147, f32[512]{0:T(512)S(1)} %bitcast.162, ...), kind=kOutput, calls=%fused_computation.1.clone.1 | convolution fusion | flops 329252864 | bytes 1323064 | tf_op jit(solution)/shard_map/while/body/eval_jaxpr/dot_general | solution.py:45
  178.0 0.3 copy.14
  178.3 1.1 constant_dynamic-update-slice_fusion.2
  179.4 0.6 dynamic_slice.8
  180.6 1.8 constant_dynamic-slice_fusion.2
  182.4 0.7 fusion.64
  183.1 18.9 %convolution_bitcast_fusion.2 = f32[1,128,2048]{1,2,0:T(8,128)S(1)} fusion(bf16[128,512]{1,0:T(8,128)(2,1)S(1)} %get-tuple-element.279, f32[]{:T(128)} %bitcast.103, f32[2048]{0:T(1024)S(1)} %bitcast.159, f32[512]{0:T(512)S(1)} %bitcast.161, f32[]{:T(128)} %bitcast.107, f32[2048]{0:T(1024)S(1)} %bitcast.147, f32[512]{0:T(512)S(1)} %bitcast.162, ...), kind=kOutput, calls=%fused_computation.1.clone.1 | convolution fusion | flops 329252864 | bytes 1323064 | tf_op jit(solution)/shard_map/while/body/eval_jaxpr/dot_general | solution.py:45
  202.1 0.3 copy.14
  202.4 1.1 constant_dynamic-update-slice_fusion.2
  203.5 0.0 reduce-scatter.4.cloned.1.call-update
  203.5 52.9 %reduce-scatter.4.cloned.1.call-done = f32[1,128,2048]{2,1,0:T(8,128)} async-done(((f32[4,128,2048]{2,1,0:T(8,128)}), f32[1,128,2048]{2,1,0:T(8,128)}) %reduce-scatter.4.cloned.1.call-update) | async-done | bytes 1048592
  256.4 2.3 bitcast_multiply_fusion
  (12 shorter events, 0.1 us)
Async XLA Ops:
  7.2 50.0 %copy-start = (f32[512,512]{1,0:T(8,128)S(1)}, f32[512,512]{1,0:T(8,128)}, u32[]{:S(2)}) copy-start(f32[512,512]{1,0:T(8,128)} %param.11) | copy-start | bytes 3145732
  7.2 52.5 %copy-start.1 = (f32[512,1024]{1,0:T(8,128)S(1)}, f32[512,1024]{1,0:T(8,128)}, u32[]{:S(2)}) copy-start(f32[512,1024]{1,0:T(8,128)} %param.10) | copy-start | bytes 6291460
  7.2 53.2 %copy-start.2 = (f32[128,512]{1,0:T(8,128)S(1)}, f32[128,512]{1,0:T(8,128)}, u32[]{:S(2)}) copy-start(f32[128,512]{1,0:T(8,128)} %param.9) | copy-start | bytes 786436
  7.2 50.0 %all-reduce.4.cloned.1.call-start = ((), (), s32[]{:S(2)}) async-start(), calls=%async_computation.1 | async-start | bytes 524288 | tf_op jit(solution)/shard_map/psum | solution.py:32
  10.1 97.2 %copy-start.3 = (f32[14]{0:T(128)S(1)}, f32[14]{0:T(128)}, u32[]{:S(2)}) copy-start(f32[14]{0:T(128)} %param.14) | copy-start | bytes 172
  10.1 97.2 %copy-start.5 = (f32[14,512]{1,0:T(8,128)S(1)}, f32[14,512]{1,0:T(8,128)}, u32[]{:S(2)}) copy-start(f32[14,512]{1,0:T(8,128)} %param.12) | copy-start | bytes 86020
  10.2 94.8 %all-reduce.6.cloned.1.call-start = ((), (), s32[]{:S(2)}) async-start(), calls=%async_computation.2 | async-start | bytes 524288 | tf_op jit(solution)/shard_map/psum | solution.py:35
  59.0 0.7 copy-start.4
  61.9 194.6 %reduce-scatter.4.cloned.1.call-start = ((), (), s32[]{:S(2)}) async-start(), calls=%async_computation.3 | async-start | bytes 5242880
  203.5 52.9 %copy-start.6 = (f32[128]{0:T(128)S(1)}, f32[128]{0:T(128)}, u32[]{:S(2)}) copy-start(f32[128]{0:T(128)} %param.15) | copy-start | bytes 1540
Sparse Core Ops, SparseCore 0:
  11.5 45.6 all-reduce.3
  62.0 42.8 all-reduce.5
  203.6 52.7 reduce-scatter.3
where the time goes:
time: 266 us; the launch traced here: 265 us
  waiting for transfers between devices  143 us (54%)
  matrix products  84.8 us (32%)
  local copies, waits for them, and re-layouts  18.5 us (7%)
  between operations  13.8 us (5%)
  loops' own time  2.73 us (1%)
    dot_general x4, matrix products, single_piece(): jnp.dot(weights_low, kernel_values(train_inputs, chosen, inv_length), pre...  75.7 us
    unnamed x4, waiting for transfers between devices  53 us
    psum x1, waiting for transfers between devices, on_device(): rest_one = lax.psum(local_one, 'rows')  47 us
    psum x1, waiting for transfers between devices, on_device(): rest_zero = lax.psum(carried, 'rows')  42.8 us
    dot_general x5, matrix products, solve_product(): jnp.dot(left, right, precision=lax.Precision.HIGHEST, preferred_element_t...  9.14 us
    slice x4, local copies, waits for them, and re-layouts, kernel_values(): query_part[dim_index][None, :]  6.93 us
    dynamic_update_slice x8, local copies, waits for them, and re-layouts, on_device(): lax.map(single_piece, jnp.arange(1 * lax.axis_size('rows'), dtype=jnp.int...  5.61 us
  transfers between devices with their start and end apart: 3, of which 3 were waited for; matrix products, arithmetic and copies ran while one was open for 0% of the time, Pallas kernels for 0%

commit v1 on v0

v1 whole, which is shorter than its diff:
```python
import functools
import math

import jax
import jax.numpy as jnp
from jax import lax
from jax.experimental import pallas as pl
from jax.experimental.pallas import tpu as pltpu
from jax.sharding import PartitionSpec as P

CHUNKS = 2
LOG2E = math.log2(math.e)
EPSILON = 1e-06 * LOG2E * LOG2E
BF16 = jnp.bfloat16
F32 = jnp.float32
SEND_TYPE = jnp.float32


def split_two(x):
    high = x.astype(BF16)
    return high, (x - high.astype(F32)).astype(BF16)


def split_three(x):
    first = x.astype(BF16).astype(F32)
    rest = x - first
    second = rest.astype(BF16).astype(F32)
    third = (rest - second).astype(BF16).astype(F32)
    return first, second, third


def product(x, high, low):
    x_high, x_low = split_two(x)
    rows = x.shape[0]
    both = jnp.dot(
        jnp.concatenate([x_high, x_low], axis=0), high, preferred_element_type=F32
    )
    return both[:rows] + (both[rows:] + jnp.dot(x_high, low, preferred_element_type=F32))


def scaled_points(points, scale):
    params, count = points.shape
    padded = -(-params // 16) * 16
    x = (points - 0.5) * scale[:params]
    return jnp.concatenate([x, jnp.zeros((padded - params, count), F32)], axis=0)


def norm_rows(x, ones_first):
    count = x.shape[1]
    n1, n2, n3 = split_three(jnp.sum(x * x, axis=0, keepdims=True))
    row = lax.broadcasted_iota(jnp.int32, (16, count), 0)
    at = 3 if ones_first else 0
    one_at = 0 if ones_first else 3
    out = jnp.where((row >= one_at) & (row < one_at + 3), 1.0, 0.0)
    out = jnp.where(row == at, n1, out)
    out = jnp.where(row == at + 1, n2, out)
    return jnp.where(row == at + 2, n3, out)


def kernel(
    rows,
    inv_ref,
    c_hbm,
    f_hbm,
    b_hbm,
    t_hbm,
    q_hbm,
    w_hbm,
    p_hbm,
    c_buf,
    f1_buf,
    f0_buf,
    b_buf,
    q_buf,
    t_all,
    h1_buf,
    l1_buf,
    h2_buf,
    l2_buf,
    part1,
    part0,
    got1,
    got0,
    got_t,
    w_buf,
    w_all,
    a_t,
    q_aug,
    k_all,
    acc,
    local_sem,
    t_send,
    t_recv,
    p1_send,
    p1_recv,
    p0_send,
    p0_recv,
    tt_send,
    tt_recv,
    c_send,
    c_recv,
    w_send,
    w_recv,
    out_sem,
):
    me = lax.axis_index("rows")
    m, block = c_buf.shape
    params, width = q_buf.shape
    step = m // CHUNKS
    tile = 512 if width % 512 == 0 else width
    tiles = width // tile

    def load(src, dst, at):
        copy = pltpu.make_async_copy(src, dst, local_sem.at[at])
        copy.start()
        return copy

    def remote(src, dst, send, recv, peer):
        return pltpu.make_async_remote_copy(
            src_ref=src,
            dst_ref=dst,
            send_sem=send,
            recv_sem=recv,
            device_id={"rows": peer},
            device_id_type=pl.DeviceIdType.MESH,
        )

    in_c = load(c_hbm, c_buf, 0)
    in_f1 = load(f_hbm.at[:, pl.ds(block, block)], f1_buf, 1)
    in_t = load(t_hbm, t_all.at[me], 2)
    in_q = load(q_hbm.at[:, pl.ds(pl.multiple_of(me * width, 128), width)], q_buf, 3)
    in_f0 = load(f_hbm.at[:, pl.ds(0, block)], f0_buf, 4)
    in_b = load(b_hbm, b_buf, 5)

    barrier = pltpu.get_barrier_semaphore()
    for k in range(1, rows):
        pl.semaphore_signal(
            barrier,
            inc=1,
            device_id={"rows": lax.rem(me + k, rows)},
            device_id_type=pl.DeviceIdType.MESH,
        )
    pl.semaphore_wait(barrier, rows - 1)

    def t_copy(k):
        return remote(
            t_hbm, t_all.at[me], t_send.at[k - 1], t_recv.at[me], lax.rem(me + k, rows)
        )

    for k in range(1, rows):
        t_copy(k).start()

    def chunk(c):
        return pl.ds(c * step, step)

    def p1_copy(c, slot):
        return remote(
            part1.at[chunk(c)],
            got1.at[slot, chunk(c)],
            p1_send.at[c],
            p1_recv.at[slot, c],
            1,
        )

    def p0_copy(c, slot):
        return remote(
            part0.at[chunk(c)],
            got0.at[slot, chunk(c)],
            p0_send.at[c],
            p0_recv.at[slot, c],
            0,
        )

    def tt_copy(c):
        return remote(
            part0.at[chunk(c)], got_t.at[chunk(c)], tt_send.at[c], tt_recv.at[c], 0
        )

    def c_copy(k):
        return remote(
            w_all.at[me],
            w_all.at[me],
            c_send.at[k - 1],
            c_recv.at[me],
            lax.rem(me + k, rows),
        )

    def w_copy(c, k):
        return remote(
            w_all.at[me, chunk(c)],
            w_all.at[me, chunk(c)],
            w_send.at[c, k - 1],
            w_recv.at[me, c],
            lax.rem(me + k, rows),
        )

    in_c.wait()
    in_f1.wait()

    @pl.when(me >= 2)
    def _():
        h1_buf[...], l1_buf[...] = split_two(f1_buf[...])
        for c in range(CHUNKS):
            part1[chunk(c)] = product(c_buf[chunk(c)], h1_buf[...], l1_buf[...]).astype(SEND_TYPE)
            p1_copy(c, me - 2).start()
        w_all[me] = c_buf[...].astype(BF16)
        for k in range(1, rows):
            c_copy(k).start()

    in_f0.wait()
    in_b.wait()
    h2_buf[...], l2_buf[...] = split_two(f0_buf[...])

    @pl.when(me >= 2)
    def _():
        for c in range(CHUNKS):
            part0[chunk(c)] = product(c_buf[chunk(c)], h2_buf[...], l2_buf[...]).astype(SEND_TYPE)
            p0_copy(c, me - 2).start()

    @pl.when(me < 2)
    def _():
        h1_buf[...], l1_buf[...] = split_two(b_buf[...])

    row = lax.broadcasted_iota(jnp.int32, (params, 1), 0)
    scale = jnp.zeros((params, 1), F32)
    for d in range(params):
        scale = jnp.where(row == d, inv_ref[d] * LOG2E, scale)
    in_q.wait()
    x = scaled_points(q_buf[...], scale)
    x1, x2, x3 = split_three(-2.0 * x)
    pieces = [x1, x2, x1, x3, x2, x1, norm_rows(x, True)]
    used = sum(piece.shape[0] for piece in pieces)
    depth = q_aug.shape[0]
    if depth > used:
        pieces.append(jnp.zeros((depth - used, width), F32))
    q_aug[...] = jnp.concatenate(pieces, axis=0).astype(BF16)

    def train_side(r):
        @pl.when(r == me)
        def _():
            in_t.wait()

        @pl.when(r != me)
        def _():
            remote(t_hbm, t_all.at[r], t_send.at[0], t_recv.at[r], 0).wait_recv()

        y = scaled_points(t_all[r], scale)
        y1, y2, y3 = split_three(y)
        parts = [y1, y1, y2, y1, y2, y3, norm_rows(y, False)]
        if depth > used:
            parts.append(jnp.zeros((depth - used, block), F32))
        a_t[...] = jnp.concatenate(parts, axis=0).T.astype(BF16)

    def kernel_tile(j):
        at = pl.ds(pl.multiple_of(j * tile, 128), tile)
        y = jnp.dot(a_t[...], q_aug[:, at], preferred_element_type=F32)
        y = jnp.maximum(y + EPSILON, EPSILON)
        return at, jnp.exp2(-(y * lax.rsqrt(y))).astype(BF16)

    for r in range(2):
        train_side(r)

        def store_tile(j, carry, r=r):
            at, values = kernel_tile(j)
            k_all[r, :, at] = values
            return carry

        lax.fori_loop(0, tiles, store_tile, 0)

    def out_copy(c):
        return pltpu.make_async_copy(w_buf.at[chunk(c)], w_hbm.at[chunk(c)], out_sem.at[c])

    @pl.when(me == 1)
    def _():
        for c in range(CHUNKS):
            rest = jnp.zeros((step, block), F32)
            for s in range(rows - 2):
                p1_copy(c, s).wait_recv()
                rest = rest + got1[s, chunk(c)].astype(F32)
            value = product(c_buf[chunk(c)] - rest, h1_buf[...], l1_buf[...])
            w_buf[chunk(c)] = value
            part0[chunk(c)] = product(value, h2_buf[...], l2_buf[...]).astype(SEND_TYPE)
            tt_copy(c).start()
            w_all[1, chunk(c)] = value.astype(BF16)
            for k in range(1, rows):
                w_copy(c, k).start()
            out_copy(c).start()

    acc[...] = jnp.zeros_like(acc)

    def later_block(r, carry):
        train_side(r)

        @pl.when(r != me)
        def _():
            remote(w_all.at[r], w_all.at[r], c_send.at[0], c_recv.at[r], 0).wait_recv()

        def add_tile(j, inner):
            at, values = kernel_tile(j)
            acc[:, at] += jnp.dot(w_all[r], values, preferred_element_type=F32)
            return inner

        return lax.fori_loop(0, tiles, add_tile, carry)

    lax.fori_loop(2, rows, later_block, 0)

    @pl.when(me == 0)
    def _():
        for c in range(CHUNKS):
            rest = jnp.zeros((step, block), F32)
            for s in range(rows - 2):
                p0_copy(c, s).wait_recv()
                rest = rest + got0[s, chunk(c)].astype(F32)
            tt_copy(c).wait_recv()
            rest = rest + got_t[chunk(c)].astype(F32)
            value = product(c_buf[chunk(c)] - rest, h1_buf[...], l1_buf[...])
            w_buf[chunk(c)] = value
            w_all[0, chunk(c)] = value.astype(BF16)
            for k in range(1, rows):
                w_copy(c, k).start()
            out_copy(c).start()

    def w_wait(r):
        @pl.when(me != r)
        def _():
            for c in range(CHUNKS):
                remote(
                    w_all.at[r, chunk(c)],
                    w_all.at[r, chunk(c)],
                    w_send.at[c, 0],
                    w_recv.at[r, c],
                    0,
                ).wait_recv()

    w_wait(1)

    def add_one(j, carry):
        at = pl.ds(pl.multiple_of(j * tile, 128), tile)
        acc[:, at] += jnp.dot(w_all[1], k_all[1, :, at], preferred_element_type=F32)
        return carry

    lax.fori_loop(0, tiles, add_one, 0)
    w_wait(0)

    def done_copy(j):
        at = pl.ds(j * tile, tile)
        return pltpu.make_async_copy(acc.at[:, at], p_hbm.at[:, at], out_sem.at[CHUNKS + j])

    for j in range(tiles):
        at = pl.ds(j * tile, tile)
        acc[:, at] += jnp.dot(w_all[0], k_all[0, :, at], preferred_element_type=F32)
        done_copy(j).start()

    for k in range(1, rows):
        t_copy(k).wait_send()

    @pl.when(me >= 2)
    def _():
        for c in range(CHUNKS):
            p1_copy(c, me - 2).wait_send()
            p0_copy(c, me - 2).wait_send()
        for k in range(1, rows):
            c_copy(k).wait_send()

    @pl.when(me == 1)
    def _():
        for c in range(CHUNKS):
            tt_copy(c).wait_send()

    @pl.when(me < 2)
    def _():
        for c in range(CHUNKS):
            for k in range(1, rows):
                w_copy(c, k).wait_send()
            out_copy(c).wait()

    for j in range(tiles):
        done_copy(j).wait()


def on_device(
    coefficients, factor_panel, block_inverse, train_inputs, query_points, inv_length, amplitude
):
    rows = lax.axis_size("rows")
    m, block = coefficients.shape
    params = train_inputs.shape[0]
    width = query_points.shape[1] // rows
    padded = -(-params // 16) * 16
    depth = -(-(6 * padded + 16) // 128) * 128
    tile = 512 if width % 512 == 0 else width
    anywhere = pl.BlockSpec(memory_space=pl.ANY)
    dma = pltpu.SemaphoreType.DMA
    vmem = pltpu.VMEM
    solved, summed = pl.pallas_call(
        functools.partial(kernel, rows),
        out_shape=(
            jax.ShapeDtypeStruct((m, block), F32),
            jax.ShapeDtypeStruct((m, width), F32),
        ),
        in_specs=[pl.BlockSpec(memory_space=pltpu.SMEM)] + [anywhere] * 5,
        out_specs=(anywhere, anywhere),
        scratch_shapes=[
            vmem((m, block), F32),
            vmem((block, block), F32),
            vmem((block, block), F32),
            vmem((block, block), F32),
            vmem((params, width), F32),
            vmem((rows, params, block), F32),
            vmem((block, block), BF16),
            vmem((block, block), BF16),
            vmem((block, block), BF16),
            vmem((block, block), BF16),
            vmem((m, block), SEND_TYPE),
            vmem((m, block), SEND_TYPE),
            vmem((rows - 2, m, block), SEND_TYPE),
            vmem((rows - 2, m, block), SEND_TYPE),
            vmem((m, block), SEND_TYPE),
            vmem((m, block), F32),
            vmem((rows, m, block), BF16),
            vmem((block, depth), BF16),
            vmem((depth, width), BF16),
            vmem((2, block, width), BF16),
            vmem((m, width), F32),
            dma((6,)),
            dma((rows - 1,)),
            dma((rows,)),
            dma((CHUNKS,)),
            dma((rows - 2, CHUNKS)),
            dma((CHUNKS,)),
            dma((rows - 2, CHUNKS)),
            dma((CHUNKS,)),
            dma((CHUNKS,)),
            dma((rows - 1,)),
            dma((rows,)),
            dma((CHUNKS, rows - 1)),
            dma((2, CHUNKS)),
            dma((CHUNKS + width // tile,)),
        ],
        compiler_params=pltpu.CompilerParams(
            collective_id=0, has_side_effects=True, vmem_limit_bytes=48 * 1024 * 1024
        ),
    )(inv_length, coefficients, factor_panel, block_inverse, train_inputs, query_points)
    weights = jnp.where(lax.axis_index("rows") < 2, solved, coefficients)
    return (weights, summed * amplitude[:, None])


def solution(mesh):
    return jax.shard_map(
        on_device,
        mesh=mesh,
        in_specs=(
            P("cols", "rows"),
            P("rows", None),
            P("rows", None),
            P(None, "rows"),
            P(),
            P(),
            P("cols"),
        ),
        out_specs=(P("cols", "rows"), P("cols", "rows")),
        check_vma=False,
    )
```

time: 266 us -> 42.2 us (0.16)
  waiting for transfers between devices: 143 us -> 0 us
  matrix products: 84.8 us -> 0 us
  Pallas kernels: 0 us -> 33.1 us
  between operations: 13.8 us -> 0.66 us
  local copies, waits for them, and re-layouts: 18.5 us -> 6.21 us
  loops' own time: 2.73 us -> 0 us
    psum x2 -> x0, waiting for transfers between devices: 89.8 us -> none  [the longest x1 47 us: on_device(): rest_one = lax.psum(local_one, 'rows')]
    dot_general x9 -> x0, matrix products: 84.8 us -> none  [the longest x4 75.7 us: single_piece(): jnp.dot(weights_low, kernel_values(train_inputs, chosen, inv_length), pre...]
    unnamed x4 -> x0, waiting for transfers between devices: 53 us -> none
    pallas_call x0 -> x1, Pallas kernels: none -> 33.1 us  [on_device(): pl.pallas_call(functools.partial(kernel, rows), out_shape=(jax.ShapeDtype...]
    slice x12 -> x0, local copies, waits for them, and re-layouts: 9.82 us -> none  [the longest x4 6.93 us: kernel_values(): query_part[dim_index][None, :]]
    dynamic_update_slice x8 -> x0, local copies, waits for them, and re-layouts: 5.61 us -> none  [on_device(): lax.map(single_piece, jnp.arange(1 * lax.axis_size('rows'), dtype=jnp.int...]
    unnamed x14, local copies, waits for them, and re-layouts: 0.73 us -> 6.21 us
    another operation x1 -> x0, loops' own time: 2.73 us -> none  [on_device(): lax.map(single_piece, jnp.arange(1 * lax.axis_size('rows'), dtype=jnp.int...]
  transfers between devices with their start and end apart: 3 -> 0, of which waited for: 3 -> 0; matrix products, arithmetic and copies ran while one was open for 0% -> 0% of each run, Pallas kernels for 0% -> 0%
where the time goes in v1:
time: 42.2 us; the launch traced here: 41.9 us
  Pallas kernels  33.1 us (78%)
  local copies, waits for them, and re-layouts  6.21 us (15%)
  other arithmetic  1.85 us (4%)
  between operations  0.66 us (2%)
    pallas_call x1, Pallas kernels, on_device(): pl.pallas_call(functools.partial(kernel, rows), out_shape=(jax.ShapeDtype...  33.1 us
    unnamed x14, local copies, waits for them, and re-layouts  6.21 us
    mul x1, other arithmetic, on_device(): return (weights, summed * amplitude[:, None])  1.11 us

profile of v1, /device:TPU:0, one launch (start us, length us, event | category | flops | bytes accessed | tf_op | source)
XLA Modules:
  0.0 41.9 jit_solution(1739132574673821407)
XLA Ops:
  0.6 0.0 copy-start
  0.6 1.6 %copy-done = f32[512,1024]{1,0:T(8,128)S(1)} copy-done((f32[512,1024]{1,0:T(8,128)S(1)}, f32[512,1024]{1,0:T(8,128)}, u32[]{:S(2)}) %copy-start) | copy-done | bytes 2097176
  2.2 0.0 copy-start.1
  2.2 0.9 %copy-done.1 = f32[128,512]{1,0:T(8,128)S(1)} copy-done((f32[128,512]{1,0:T(8,128)S(1)}, f32[128,512]{1,0:T(8,128)}, u32[]{:S(2)}) %copy-start.1) | copy-done | bytes 262168
  3.2 0.0 copy-start.2
  3.2 1.2 %copy-done.2 = f32[512,512]{1,0:T(8,128)S(1)} copy-done((f32[512,512]{1,0:T(8,128)S(1)}, f32[512,512]{1,0:T(8,128)}, u32[]{:S(2)}) %copy-start.2) | copy-done | bytes 1048600
  4.4 0.0 copy-start.3
  4.4 1.0 %copy-done.3 = f32[14,8192]{1,0:T(8,128)S(1)} copy-done((f32[14,8192]{1,0:T(8,128)S(1)}, f32[14,8192]{1,0:T(8,128)}, u32[]{:S(2)}) %copy-start.3) | copy-done | bytes 458776
  5.4 0.0 copy-start.4
  5.5 0.8 %copy-done.4 = f32[14,512]{1,0:T(8,128)S(1)} copy-done((f32[14,512]{1,0:T(8,128)S(1)}, f32[14,512]{1,0:T(8,128)}, u32[]{:S(2)}) %copy-start.4) | copy-done | bytes 28696
  6.2 0.0 copy-start.5
  6.2 0.7 %copy-done.5 = f32[14]{0:T(128)S(1)} copy-done((f32[14]{0:T(128)S(1)}, f32[14]{0:T(128)}, u32[]{:S(2)}) %copy-start.5) | copy-done | bytes 80
  6.9 0.0 copy-start.6
  6.9 33.1 %shard_map.86 = (f32[128,512]{1,0:T(8,128)S(1)}, f32[128,2048]{1,0:T(8,128)S(1)}) custom-call(f32[14]{0:T(128)S(1)} %copy-done.5, f32[128,512]{1,0:T(8,128)S(1)} %copy-done.1, f32[512,1024]{1,0:T(8,128)S(1)} %copy-done, f32[512,512]{1,0:T(8,128)S(1)} %copy-done.2, f32[14,512]{1,0:T(8,128)S(1)} %copy-done.4, f32[14,8192]{1,0:T(8,128)S(1)} %copy-done.3), custom_call_target="tpu_custom_call" | custom-call | tf_op jit(solution)/shard_map/pallas_call | solution.py:394
  40.0 0.7 %broadcast_select_fusion = f32[128,512]{1,0:T(8,128)} fusion(f32[128,512]{1,0:T(8,128)S(1)} %get-tuple-element.4, f32[128,512]{1,0:T(8,128)S(1)} %copy-done.1, pred[]{:T(512)S(6)} %lt.3), kind=kLoop, calls=%fused_computation.1 | loop fusion | flops 65536 | bytes 786433 | tf_op jit(solution)/shard_map/jit(_where)/select_n | solution.py:443
  40.8 0.0 copy-done.6
  40.8 1.1 %broadcast_multiply_fusion = f32[128,2048]{1,0:T(8,128)} fusion(f32[128,2048]{1,0:T(8,128)S(1)} %get-tuple-element.5, f32[128]{0:T(128)S(1)} %copy-done.6), kind=kLoop, calls=%fused_computation | loop fusion | flops 262144 | bytes 2097664 | tf_op jit(solution)/shard_map/mul | solution.py:444
Async XLA Ops:
  0.6 1.6 %copy-start = (f32[512,1024]{1,0:T(8,128)S(1)}, f32[512,1024]{1,0:T(8,128)}, u32[]{:S(2)}) copy-start(f32[512,1024]{1,0:T(8,128)} %f_hbm.1) | copy-start | bytes 6291460
  2.2 0.9 %copy-start.1 = (f32[128,512]{1,0:T(8,128)S(1)}, f32[128,512]{1,0:T(8,128)}, u32[]{:S(2)}) copy-start(f32[128,512]{1,0:T(8,128)} %c_hbm.1) | copy-start | bytes 786436
  3.2 1.2 %copy-start.2 = (f32[512,512]{1,0:T(8,128)S(1)}, f32[512,512]{1,0:T(8,128)}, u32[]{:S(2)}) copy-start(f32[512,512]{1,0:T(8,128)} %b_hbm.1) | copy-start | bytes 3145732
  4.4 1.0 %copy-start.3 = (f32[14,8192]{1,0:T(8,128)S(1)}, f32[14,8192]{1,0:T(8,128)}, u32[]{:S(2)}) copy-start(f32[14,8192]{1,0:T(8,128)} %q_hbm.1) | copy-start | bytes 1376260
  5.4 0.8 %copy-start.4 = (f32[14,512]{1,0:T(8,128)S(1)}, f32[14,512]{1,0:T(8,128)}, u32[]{:S(2)}) copy-start(f32[14,512]{1,0:T(8,128)} %t_hbm.1) | copy-start | bytes 86020
  6.2 0.7 %copy-start.5 = (f32[14]{0:T(128)S(1)}, f32[14]{0:T(128)}, u32[]{:S(2)}) copy-start(f32[14]{0:T(128)} %inv_ref.1) | copy-start | bytes 172
  6.9 33.9 %copy-start.6 = (f32[128]{0:T(128)S(1)}, f32[128]{0:T(128)}, u32[]{:S(2)}) copy-start(f32[128]{0:T(128)} %param.13) | copy-start | bytes 1540

commit v2 on v1

--- a/solution.py
+++ b/solution.py
@@ -8,12 +8,12 @@
 from jax.experimental.pallas import tpu as pltpu
 from jax.sharding import PartitionSpec as P
 
-CHUNKS = 2
+CHUNKS = 4
 LOG2E = math.log2(math.e)
 EPSILON = 1e-06 * LOG2E * LOG2E
 BF16 = jnp.bfloat16
 F32 = jnp.float32
-SEND_TYPE = jnp.float32
+SEND_TYPE = jnp.bfloat16
 
 
 def split_two(x):
@@ -200,12 +200,12 @@
     @pl.when(me >= 2)
     def _():
         h1_buf[...], l1_buf[...] = split_two(f1_buf[...])
-        for c in range(CHUNKS):
-            part1[chunk(c)] = product(c_buf[chunk(c)], h1_buf[...], l1_buf[...]).astype(SEND_TYPE)
-            p1_copy(c, me - 2).start()
+        for half in range(2):
+            at = pl.ds(half * m // 2, m // 2)
+            part1[at] = product(c_buf[at], h1_buf[...], l1_buf[...]).astype(SEND_TYPE)
+            for c in range(half * CHUNKS // 2, (half + 1) * CHUNKS // 2):
+                p1_copy(c, me - 2).start()
         w_all[me] = c_buf[...].astype(BF16)
-        for k in range(1, rows):
-            c_copy(k).start()
 
     in_f0.wait()
     in_b.wait()
@@ -213,8 +213,8 @@
 
     @pl.when(me >= 2)
     def _():
-        for c in range(CHUNKS):
-            part0[chunk(c)] = product(c_buf[chunk(c)], h2_buf[...], l2_buf[...]).astype(SEND_TYPE)
+        part0[...] = product(c_buf[...], h2_buf[...], l2_buf[...]).astype(SEND_TYPE)
+        for c in range(CHUNKS):
             p0_copy(c, me - 2).start()
 
     @pl.when(me < 2)
@@ -257,15 +257,22 @@
         y = jnp.maximum(y + EPSILON, EPSILON)
         return at, jnp.exp2(-(y * lax.rsqrt(y))).astype(BF16)
 
-    for r in range(2):
+    def kernel_block(r, carry):
         train_side(r)
 
-        def store_tile(j, carry, r=r):
+        def store_tile(j, inner):
             at, values = kernel_tile(j)
             k_all[r, :, at] = values
-            return carry
-
-        lax.fori_loop(0, tiles, store_tile, 0)
+            return inner
+
+        return lax.fori_loop(0, tiles, store_tile, carry)
+
+    lax.fori_loop(0, 2, kernel_block, 0)
+
+    @pl.when(me >= 2)
+    def _():
+        for k in range(1, rows):
+            c_copy(k).start()
 
     def out_copy(c):
         return pltpu.make_async_copy(w_buf.at[chunk(c)], w_hbm.at[chunk(c)], out_sem.at[c])
@@ -282,27 +289,12 @@
             part0[chunk(c)] = product(value, h2_buf[...], l2_buf[...]).astype(SEND_TYPE)
             tt_copy(c).start()
             w_all[1, chunk(c)] = value.astype(BF16)
+            out_copy(c).start()
+        for c in range(CHUNKS):
             for k in range(1, rows):
                 w_copy(c, k).start()
-            out_copy(c).start()
-
-    acc[...] = jnp.zeros_like(acc)
-
-    def later_block(r, carry):
-        train_side(r)
-
-        @pl.when(r != me)
-        def _():
-            remote(w_all.at[r], w_all.at[r], c_send.at[0], c_recv.at[r], 0).wait_recv()
-
-        def add_tile(j, inner):
-            at, values = kernel_tile(j)
-            acc[:, at] += jnp.dot(w_all[r], values, preferred_element_type=F32)
-            return inner
-
-        return lax.fori_loop(0, tiles, add_tile, carry)
-
-    lax.fori_loop(2, rows, later_block, 0)
+
+    lax.fori_loop(2, rows, kernel_block, 0)
 
     @pl.when(me == 0)
     def _():
@@ -320,6 +312,26 @@
                 w_copy(c, k).start()
             out_copy(c).start()
 
+    acc[...] = jnp.zeros_like(acc)
+
+    def add_block(r):
+        def add_tile(j, carry):
+            at = pl.ds(pl.multiple_of(j * tile, 128), tile)
+            acc[:, at] += jnp.dot(w_all[r], k_all[r, :, at], preferred_element_type=F32)
+            return carry
+
+        lax.fori_loop(0, tiles, add_tile, 0)
+
+    def later_block(r, carry):
+        @pl.when(r != me)
+        def _():
+            remote(w_all.at[r], w_all.at[r], c_send.at[0], c_recv.at[r], 0).wait_recv()
+
+        add_block(r)
+        return carry
+
+    lax.fori_loop(2, rows, later_block, 0)
+
     def w_wait(r):
         @pl.when(me != r)
         def _():
@@ -334,12 +346,7 @@
 
     w_wait(1)
 
-    def add_one(j, carry):
-        at = pl.ds(pl.multiple_of(j * tile, 128), tile)
-        acc[:, at] += jnp.dot(w_all[1], k_all[1, :, at], preferred_element_type=F32)
-        return carry
-
-    lax.fori_loop(0, tiles, add_one, 0)
+    add_block(1)
     w_wait(0)
 
     def done_copy(j):
@@ -388,7 +395,7 @@
     padded = -(-params // 16) * 16
     depth = -(-(6 * padded + 16) // 128) * 128
     tile = 512 if width % 512 == 0 else width
-    anywhere = pl.BlockSpec(memory_space=pl.ANY)
+    anywhere = pl.BlockSpec(memory_space=pltpu.HBM)
     dma = pltpu.SemaphoreType.DMA
     vmem = pltpu.VMEM
     solved, summed = pl.pallas_call(
@@ -419,7 +426,7 @@
             vmem((rows, m, block), BF16),
             vmem((block, depth), BF16),
             vmem((depth, width), BF16),
-            vmem((2, block, width), BF16),
+            vmem((rows, block, width), BF16),
             vmem((m, width), F32),
             dma((6,)),
             dma((rows - 1,)),
@@ -437,7 +444,7 @@
             dma((CHUNKS + width // tile,)),
         ],
         compiler_params=pltpu.CompilerParams(
-            collective_id=0, has_side_effects=True, vmem_limit_bytes=48 * 1024 * 1024
+            collective_id=0, has_side_effects=True, vmem_limit_bytes=60 * 1024 * 1024
         ),
     )(inv_length, coefficients, factor_panel, block_inverse, train_inputs, query_points)
     weights = jnp.where(lax.axis_index("rows") < 2, solved, coefficients)

time: 42.2 us -> 30.2 us (0.72)
  Pallas kernels: 33.1 us -> 25.3 us
  local copies, waits for them, and re-layouts: 6.21 us -> 0.01 us
  other arithmetic: 1.85 us -> 4.03 us
    pallas_call x1, Pallas kernels: 33.1 us -> 25.3 us  [on_device(): pl.pallas_call(functools.partial(kernel, rows), out_shape=(jax.ShapeDtype...]
    unnamed x14 -> x4, local copies, waits for them, and re-layouts: 6.21 us -> 0.01 us
    mul x1, other arithmetic: 1.11 us -> 2.33 us  [on_device(): return (weights, summed * amplitude[:, None])]
    select_n x1, other arithmetic: 0.74 us -> 1.7 us  [on_device(): weights = jnp.where(lax.axis_index('rows') < 2, solved, coefficients)]
where the time goes in v2:
time: 30.2 us; the launch traced here: 30 us
  Pallas kernels  25.3 us (84%)
  other arithmetic  4.03 us (13%)
  between operations  0.67 us (2%)
    pallas_call x1, Pallas kernels, on_device(): pl.pallas_call(functools.partial(kernel, rows), out_shape=(jax.ShapeDtype...  25.3 us
    mul x1, other arithmetic, on_device(): return (weights, summed * amplitude[:, None])  2.33 us
    select_n x1, other arithmetic, on_device(): weights = jnp.where(lax.axis_index('rows') < 2, solved, coefficients)  1.7 us

profile of v2, /device:TPU:0, one launch (start us, length us, event | category | flops | bytes accessed | tf_op | source)
XLA Modules:
  0.0 30.0 jit_solution(14715417787803403011)
XLA Ops:
  0.6 0.0 copy-start
  0.6 0.0 copy-start.1
  0.7 25.3 %shard_map.86 = (f32[128,512]{1,0:T(8,128)}, f32[128,2048]{1,0:T(8,128)}) custom-call(f32[14]{0:T(128)} %inv_ref.1, f32[128,512]{1,0:T(8,128)} %c_hbm.1, f32[512,1024]{1,0:T(8,128)} %f_hbm.1, f32[512,512]{1,0:T(8,128)} %b_hbm.1, f32[14,512]{1,0:T(8,128)} %t_hbm.1, f32[14,8192]{1,0:T(8,128)} %q_hbm.1), custom_call_target="tpu_custom_call" | custom-call | tf_op jit(solution)/shard_map/pallas_call | solution.py:401
  26.0 0.0 copy-done
  26.0 1.7 %broadcast_select_fusion = f32[128,512]{1,0:T(8,128)} fusion(f32[128,512]{1,0:T(8,128)} %get-tuple-element.4, f32[128,512]{1,0:T(8,128)S(1)} %copy-done, pred[]{:T(512)S(6)} %lt.3), kind=kLoop, calls=%fused_computation.1 | loop fusion | flops 65536 | bytes 786433 | tf_op jit(solution)/shard_map/jit(_where)/select_n | solution.py:450
  27.7 0.0 copy-done.1
  27.7 2.3 %broadcast_multiply_fusion = f32[128,2048]{1,0:T(8,128)} fusion(f32[128,2048]{1,0:T(8,128)} %get-tuple-element.5, f32[128]{0:T(128)S(1)} %copy-done.1), kind=kLoop, calls=%fused_computation | loop fusion | flops 262144 | bytes 2097664 | tf_op jit(solution)/shard_map/mul | solution.py:451
Async XLA Ops:
  0.6 25.3 %copy-start = (f32[128,512]{1,0:T(8,128)S(1)}, f32[128,512]{1,0:T(8,128)}, u32[]{:S(2)}) copy-start(f32[128,512]{1,0:T(8,128)} %c_hbm.1) | copy-start | bytes 786436
  0.6 27.0 %copy-start.1 = (f32[128]{0:T(128)S(1)}, f32[128]{0:T(128)}, u32[]{:S(2)}) copy-start(f32[128]{0:T(128)} %param.13) | copy-start | bytes 1540

commit v3 on v2

--- a/solution.py
+++ b/solution.py
@@ -65,8 +65,8 @@
     b_hbm,
     t_hbm,
     q_hbm,
-    w_hbm,
-    p_hbm,
+    w_buf,
+    acc,
     c_buf,
     f1_buf,
     f0_buf,
@@ -82,12 +82,10 @@
     got1,
     got0,
     got_t,
-    w_buf,
     w_all,
     a_t,
     q_aug,
     k_all,
-    acc,
     local_sem,
     t_send,
     t_recv,
@@ -101,7 +99,6 @@
     c_recv,
     w_send,
     w_recv,
-    out_sem,
 ):
     me = lax.axis_index("rows")
     m, block = c_buf.shape
@@ -274,9 +271,6 @@
         for k in range(1, rows):
             c_copy(k).start()
 
-    def out_copy(c):
-        return pltpu.make_async_copy(w_buf.at[chunk(c)], w_hbm.at[chunk(c)], out_sem.at[c])
-
     @pl.when(me == 1)
     def _():
         for c in range(CHUNKS):
@@ -289,12 +283,31 @@
             part0[chunk(c)] = product(value, h2_buf[...], l2_buf[...]).astype(SEND_TYPE)
             tt_copy(c).start()
             w_all[1, chunk(c)] = value.astype(BF16)
-            out_copy(c).start()
         for c in range(CHUNKS):
             for k in range(1, rows):
                 w_copy(c, k).start()
 
     lax.fori_loop(2, rows, kernel_block, 0)
+
+    acc[...] = jnp.zeros_like(acc)
+
+    def add_block(r):
+        def add_tile(j, carry):
+            at = pl.ds(pl.multiple_of(j * tile, 128), tile)
+            acc[:, at] += jnp.dot(w_all[r], k_all[r, :, at], preferred_element_type=F32)
+            return carry
+
+        lax.fori_loop(0, tiles, add_tile, 0)
+
+    def later_block(r, carry):
+        @pl.when(r != me)
+        def _():
+            remote(w_all.at[r], w_all.at[r], c_send.at[0], c_recv.at[r], 0).wait_recv()
+
+        add_block(r)
+        return carry
+
+    lax.fori_loop(2, rows, later_block, 0)
 
     @pl.when(me == 0)
     def _():
@@ -310,27 +323,6 @@
             w_all[0, chunk(c)] = value.astype(BF16)
             for k in range(1, rows):
                 w_copy(c, k).start()
-            out_copy(c).start()
-
-    acc[...] = jnp.zeros_like(acc)
-
-    def add_block(r):
-        def add_tile(j, carry):
-            at = pl.ds(pl.multiple_of(j * tile, 128), tile)
-            acc[:, at] += jnp.dot(w_all[r], k_all[r, :, at], preferred_element_type=F32)
-            return carry
-
-        lax.fori_loop(0, tiles, add_tile, 0)
-
-    def later_block(r, carry):
-        @pl.when(r != me)
-        def _():
-            remote(w_all.at[r], w_all.at[r], c_send.at[0], c_recv.at[r], 0).wait_recv()
-
-        add_block(r)
-        return carry
-
-    lax.fori_loop(2, rows, later_block, 0)
 
     def w_wait(r):
         @pl.when(me != r)
@@ -349,14 +341,7 @@
     add_block(1)
     w_wait(0)
 
-    def done_copy(j):
-        at = pl.ds(j * tile, tile)
-        return pltpu.make_async_copy(acc.at[:, at], p_hbm.at[:, at], out_sem.at[CHUNKS + j])
-
-    for j in range(tiles):
-        at = pl.ds(j * tile, tile)
-        acc[:, at] += jnp.dot(w_all[0], k_all[0, :, at], preferred_element_type=F32)
-        done_copy(j).start()
+    add_block(0)
 
     for k in range(1, rows):
         t_copy(k).wait_send()
@@ -379,10 +364,6 @@
         for c in range(CHUNKS):
             for k in range(1, rows):
                 w_copy(c, k).wait_send()
-            out_copy(c).wait()
-
-    for j in range(tiles):
-        done_copy(j).wait()
 
 
 def on_device(
@@ -394,18 +375,17 @@
     width = query_points.shape[1] // rows
     padded = -(-params // 16) * 16
     depth = -(-(6 * padded + 16) // 128) * 128
-    tile = 512 if width % 512 == 0 else width
     anywhere = pl.BlockSpec(memory_space=pltpu.HBM)
     dma = pltpu.SemaphoreType.DMA
     vmem = pltpu.VMEM
     solved, summed = pl.pallas_call(
         functools.partial(kernel, rows),
         out_shape=(
-            jax.ShapeDtypeStruct((m, block), F32),
-            jax.ShapeDtypeStruct((m, width), F32),
+            pltpu.VMEM((m, block), F32),
+            pltpu.VMEM((m, width), F32),
         ),
         in_specs=[pl.BlockSpec(memory_space=pltpu.SMEM)] + [anywhere] * 5,
-        out_specs=(anywhere, anywhere),
+        out_specs=(pl.BlockSpec(memory_space=pltpu.VMEM),) * 2,
         scratch_shapes=[
             vmem((m, block), F32),
             vmem((block, block), F32),
@@ -422,12 +402,10 @@
             vmem((rows - 2, m, block), SEND_TYPE),
             vmem((rows - 2, m, block), SEND_TYPE),
             vmem((m, block), SEND_TYPE),
-            vmem((m, block), F32),
             vmem((rows, m, block), BF16),
             vmem((block, depth), BF16),
             vmem((depth, width), BF16),
             vmem((rows, block, width), BF16),
-            vmem((m, width), F32),
             dma((6,)),
             dma((rows - 1,)),
             dma((rows,)),
@@ -441,7 +419,6 @@
             dma((rows,)),
             dma((CHUNKS, rows - 1)),
             dma((2, CHUNKS)),
-            dma((CHUNKS + width // tile,)),
         ],
         compiler_params=pltpu.CompilerParams(
             collective_id=0, has_side_effects=True, vmem_limit_bytes=60 * 1024 * 1024

time: 30.2 us -> 30.6 us (1.013)
  the two profiles are of different devices: /device:TPU:0 before, /device:TPU:30 now
where the time goes in v3:
time: 30.6 us; the launch traced here: 30.4 us
  Pallas kernels  27.9 us (91%)
  other arithmetic  1.85 us (6%)
  between operations  0.67 us (2%)
    pallas_call x1, Pallas kernels, on_device(): pl.pallas_call(functools.partial(kernel, rows), out_shape=(pltpu.VMEM((m,...  27.9 us
    mul x1, other arithmetic, on_device(): return (weights, summed * amplitude[:, None])  1.11 us
    select_n x1, other arithmetic, on_device(): weights = jnp.where(lax.axis_index('rows') < 2, solved, coefficients)  0.74 us

profile of v3, /device:TPU:30, one launch (start us, length us, event | category | flops | bytes accessed | tf_op | source)
XLA Modules:
  0.0 30.4 jit_solution(15454371936769503816)
XLA Ops:
  0.6 0.0 copy-start
  0.6 0.0 copy-start.1
  0.7 27.9 %shard_map.86 = (f32[128,512]{1,0:T(8,128)S(1)}, f32[128,2048]{1,0:T(8,128)S(1)}) custom-call(f32[14]{0:T(128)} %inv_ref.1, f32[128,512]{1,0:T(8,128)} %c_hbm.1, f32[512,1024]{1,0:T(8,128)} %f_hbm.1, f32[512,512]{1,0:T(8,128)} %b_hbm.1, f32[14,512]{1,0:T(8,128)} %t_hbm.1, f32[14,8192]{1,0:T(8,128)} %q_hbm.1), custom_call_target="tpu_custom_call" | custom-call | tf_op jit(solution)/shard_map/pallas_call | solution.py:381
  28.5 0.0 copy-done
  28.5 0.7 %broadcast_select_fusion = f32[128,512]{1,0:T(8,128)} fusion(f32[128,512]{1,0:T(8,128)S(1)} %get-tuple-element.4, f32[128,512]{1,0:T(8,128)S(1)} %copy-done, pred[]{:T(512)S(6)} %lt.3), kind=kLoop, calls=%fused_computation.1 | loop fusion | flops 65536 | bytes 786433 | tf_op jit(solution)/shard_map/jit(_where)/select_n | solution.py:427
  29.3 0.0 copy-done.1
  29.3 1.1 %broadcast_multiply_fusion = f32[128,2048]{1,0:T(8,128)} fusion(f32[128,2048]{1,0:T(8,128)S(1)} %get-tuple-element.5, f32[128]{0:T(128)S(1)} %copy-done.1), kind=kLoop, calls=%fused_computation | loop fusion | flops 262144 | bytes 2097664 | tf_op jit(solution)/shard_map/mul | solution.py:428
Async XLA Ops:
  0.6 27.9 %copy-start = (f32[128,512]{1,0:T(8,128)S(1)}, f32[128,512]{1,0:T(8,128)}, u32[]{:S(2)}) copy-start(f32[128,512]{1,0:T(8,128)} %c_hbm.1) | copy-start | bytes 786436
  0.6 28.6 %copy-start.1 = (f32[128]{0:T(128)S(1)}, f32[128]{0:T(128)}, u32[]{:S(2)}) copy-start(f32[128]{0:T(128)} %param.13) | copy-start | bytes 1540

commit v4 on v3

--- a/solution.py
+++ b/solution.py
@@ -1,5 +1,4 @@
 import functools
-import math
 
 import jax
 import jax.numpy as jnp
@@ -9,8 +8,7 @@
 from jax.sharding import PartitionSpec as P
 
 CHUNKS = 4
-LOG2E = math.log2(math.e)
-EPSILON = 1e-06 * LOG2E * LOG2E
+EPSILON = 1e-06
 BF16 = jnp.bfloat16
 F32 = jnp.float32
 SEND_TYPE = jnp.bfloat16
@@ -45,9 +43,9 @@
     return jnp.concatenate([x, jnp.zeros((padded - params, count), F32)], axis=0)
 
 
-def norm_rows(x, ones_first):
+def norm_rows(x, ones_first, added):
     count = x.shape[1]
-    n1, n2, n3 = split_three(jnp.sum(x * x, axis=0, keepdims=True))
+    n1, n2, n3 = split_three(jnp.sum(x * x, axis=0, keepdims=True) + added)
     row = lax.broadcasted_iota(jnp.int32, (16, count), 0)
     at = 3 if ones_first else 0
     one_at = 0 if ones_first else 3
@@ -150,6 +148,9 @@
     def chunk(c):
         return pl.ds(c * step, step)
 
+    def part(r):
+        return pl.ds(pl.multiple_of(r * block, block), block)
+
     def p1_copy(c, slot):
         return remote(
             part1.at[chunk(c)],
@@ -175,8 +176,8 @@
 
     def c_copy(k):
         return remote(
-            w_all.at[me],
-            w_all.at[me],
+            w_all.at[:, part(me)],
+            w_all.at[:, part(me)],
             c_send.at[k - 1],
             c_recv.at[me],
             lax.rem(me + k, rows),
@@ -184,8 +185,8 @@
 
     def w_copy(c, k):
         return remote(
-            w_all.at[me, chunk(c)],
-            w_all.at[me, chunk(c)],
+            w_all.at[chunk(c), part(me)],
+            w_all.at[chunk(c), part(me)],
             w_send.at[c, k - 1],
             w_recv.at[me, c],
             lax.rem(me + k, rows),
@@ -202,7 +203,7 @@
             part1[at] = product(c_buf[at], h1_buf[...], l1_buf[...]).astype(SEND_TYPE)
             for c in range(half * CHUNKS // 2, (half + 1) * CHUNKS // 2):
                 p1_copy(c, me - 2).start()
-        w_all[me] = c_buf[...].astype(BF16)
+        w_all[:, part(me)] = c_buf[...].astype(BF16)
 
     in_f0.wait()
     in_b.wait()
@@ -221,11 +222,11 @@
     row = lax.broadcasted_iota(jnp.int32, (params, 1), 0)
     scale = jnp.zeros((params, 1), F32)
     for d in range(params):
-        scale = jnp.where(row == d, inv_ref[d] * LOG2E, scale)
+        scale = jnp.where(row == d, inv_ref[d], scale)
     in_q.wait()
     x = scaled_points(q_buf[...], scale)
     x1, x2, x3 = split_three(-2.0 * x)
-    pieces = [x1, x2, x1, x3, x2, x1, norm_rows(x, True)]
+    pieces = [x1, x2, x1, x3, x2, x1, norm_rows(x, True, EPSILON)]
     used = sum(piece.shape[0] for piece in pieces)
     depth = q_aug.shape[0]
     if depth > used:
@@ -243,7 +244,7 @@
 
         y = scaled_points(t_all[r], scale)
         y1, y2, y3 = split_three(y)
-        parts = [y1, y1, y2, y1, y2, y3, norm_rows(y, False)]
+        parts = [y1, y1, y2, y1, y2, y3, norm_rows(y, False, 0.0)]
         if depth > used:
             parts.append(jnp.zeros((depth - used, block), F32))
         a_t[...] = jnp.concatenate(parts, axis=0).T.astype(BF16)
@@ -251,15 +252,15 @@
     def kernel_tile(j):
         at = pl.ds(pl.multiple_of(j * tile, 128), tile)
         y = jnp.dot(a_t[...], q_aug[:, at], preferred_element_type=F32)
-        y = jnp.maximum(y + EPSILON, EPSILON)
-        return at, jnp.exp2(-(y * lax.rsqrt(y))).astype(BF16)
+        y = jnp.maximum(y, EPSILON)
+        return at, jnp.exp(-(y * lax.rsqrt(y))).astype(BF16)
 
     def kernel_block(r, carry):
         train_side(r)
 
         def store_tile(j, inner):
             at, values = kernel_tile(j)
-            k_all[r, :, at] = values
+            k_all[part(r), at] = values
             return inner
 
         return lax.fori_loop(0, tiles, store_tile, carry)
@@ -282,32 +283,12 @@
             w_buf[chunk(c)] = value
             part0[chunk(c)] = product(value, h2_buf[...], l2_buf[...]).astype(SEND_TYPE)
             tt_copy(c).start()
-            w_all[1, chunk(c)] = value.astype(BF16)
+            w_all[chunk(c), part(1)] = value.astype(BF16)
         for c in range(CHUNKS):
             for k in range(1, rows):
                 w_copy(c, k).start()
 
     lax.fori_loop(2, rows, kernel_block, 0)
-
-    acc[...] = jnp.zeros_like(acc)
-
-    def add_block(r):
-        def add_tile(j, carry):
-            at = pl.ds(pl.multiple_of(j * tile, 128), tile)
-            acc[:, at] += jnp.dot(w_all[r], k_all[r, :, at], preferred_element_type=F32)
-            return carry
-
-        lax.fori_loop(0, tiles, add_tile, 0)
-
-    def later_block(r, carry):
-        @pl.when(r != me)
-        def _():
-            remote(w_all.at[r], w_all.at[r], c_send.at[0], c_recv.at[r], 0).wait_recv()
-
-        add_block(r)
-        return carry
-
-    lax.fori_loop(2, rows, later_block, 0)
 
     @pl.when(me == 0)
     def _():
@@ -320,7 +301,7 @@
             rest = rest + got_t[chunk(c)].astype(F32)
             value = product(c_buf[chunk(c)] - rest, h1_buf[...], l1_buf[...])
             w_buf[chunk(c)] = value
-            w_all[0, chunk(c)] = value.astype(BF16)
+            w_all[chunk(c), part(0)] = value.astype(BF16)
             for k in range(1, rows):
                 w_copy(c, k).start()
 
@@ -329,19 +310,43 @@
         def _():
             for c in range(CHUNKS):
                 remote(
-                    w_all.at[r, chunk(c)],
-                    w_all.at[r, chunk(c)],
+                    w_all.at[chunk(c), part(r)],
+                    w_all.at[chunk(c), part(r)],
                     w_send.at[c, 0],
                     w_recv.at[r, c],
                     0,
                 ).wait_recv()
 
+    def later_block(r, carry):
+        @pl.when(r != me)
+        def _():
+            remote(
+                w_all.at[:, part(r)], w_all.at[:, part(r)], c_send.at[0], c_recv.at[r], 0
+            ).wait_recv()
+
+        return carry
+
+    lax.fori_loop(2, rows, later_block, 0)
     w_wait(1)
 
-    add_block(1)
+    def first_tile(j, carry):
+        at = pl.ds(pl.multiple_of(j * tile, 128), tile)
+        acc[:, at] = jnp.dot(
+            w_all[:, block:], k_all[block:, at], preferred_element_type=F32
+        )
+        return carry
+
+    lax.fori_loop(0, tiles, first_tile, 0)
     w_wait(0)
 
-    add_block(0)
+    def last_tile(j, carry):
+        at = pl.ds(pl.multiple_of(j * tile, 128), tile)
+        acc[:, at] += jnp.dot(
+            w_all[:, :block], k_all[:block, at], preferred_element_type=F32
+        )
+        return carry
+
+    lax.fori_loop(0, tiles, last_tile, 0)
 
     for k in range(1, rows):
         t_copy(k).wait_send()
@@ -402,10 +407,10 @@
             vmem((rows - 2, m, block), SEND_TYPE),
             vmem((rows - 2, m, block), SEND_TYPE),
             vmem((m, block), SEND_TYPE),
-            vmem((rows, m, block), BF16),
+            vmem((m, rows * block), BF16),
             vmem((block, depth), BF16),
             vmem((depth, width), BF16),
-            vmem((rows, block, width), BF16),
+            vmem((rows * block, width), BF16),
             dma((6,)),
             dma((rows - 1,)),
             dma((rows,)),

time: 30.6 us -> 28.4 us (0.928)
  the two profiles are of different devices: /device:TPU:30 before, /device:TPU:0 now
where the time goes in v4:
time: 28.4 us; the launch traced here: 28.2 us
  Pallas kernels  25.7 us (90%)
  other arithmetic  1.85 us (7%)
  between operations  0.67 us (2%)
    pallas_call x1, Pallas kernels, on_device(): pl.pallas_call(functools.partial(kernel, rows), out_shape=(pltpu.VMEM((m,...  25.7 us
    mul x1, other arithmetic, on_device(): return (weights, summed * amplitude[:, None])  1.11 us
    select_n x1, other arithmetic, on_device(): weights = jnp.where(lax.axis_index('rows') < 2, solved, coefficients)  0.74 us

profile of v4, /device:TPU:0, one launch (start us, length us, event | category | flops | bytes accessed | tf_op | source)
XLA Modules:
  0.0 28.2 jit_solution(6400526677425579977)
XLA Ops:
  0.6 0.0 copy-start
  0.6 0.0 copy-start.1
  0.7 25.7 %shard_map.86 = (f32[128,512]{1,0:T(8,128)S(1)}, f32[128,2048]{1,0:T(8,128)S(1)}) custom-call(f32[14]{0:T(128)} %inv_ref.1, f32[128,512]{1,0:T(8,128)} %c_hbm.1, f32[512,1024]{1,0:T(8,128)} %f_hbm.1, f32[512,512]{1,0:T(8,128)} %b_hbm.1, f32[14,512]{1,0:T(8,128)} %t_hbm.1, f32[14,8192]{1,0:T(8,128)} %q_hbm.1), custom_call_target="tpu_custom_call" | custom-call | tf_op jit(solution)/shard_map/pallas_call | solution.py:386
  26.3 0.0 copy-done
  26.4 0.7 %broadcast_select_fusion = f32[128,512]{1,0:T(8,128)} fusion(f32[128,512]{1,0:T(8,128)S(1)} %get-tuple-element.4, f32[128,512]{1,0:T(8,128)S(1)} %copy-done, pred[]{:T(512)S(6)} %lt.3), kind=kLoop, calls=%fused_computation.1 | loop fusion | flops 65536 | bytes 786433 | tf_op jit(solution)/shard_map/jit(_where)/select_n | solution.py:432
  27.1 0.0 copy-done.1
  27.1 1.1 %broadcast_multiply_fusion = f32[128,2048]{1,0:T(8,128)} fusion(f32[128,2048]{1,0:T(8,128)S(1)} %get-tuple-element.5, f32[128]{0:T(128)S(1)} %copy-done.1), kind=kLoop, calls=%fused_computation | loop fusion | flops 262144 | bytes 2097664 | tf_op jit(solution)/shard_map/mul | solution.py:433
Async XLA Ops:
  0.6 25.7 %copy-start = (f32[128,512]{1,0:T(8,128)S(1)}, f32[128,512]{1,0:T(8,128)}, u32[]{:S(2)}) copy-start(f32[128,512]{1,0:T(8,128)} %c_hbm.1) | copy-start | bytes 786436
  0.6 26.4 %copy-start.1 = (f32[128]{0:T(128)S(1)}, f32[128]{0:T(128)}, u32[]{:S(2)}) copy-start(f32[128]{0:T(128)} %param.13) | copy-start | bytes 1540

commit v5 on v4

--- a/solution.py
+++ b/solution.py
@@ -64,7 +64,7 @@
     t_hbm,
     q_hbm,
     w_buf,
-    acc,
+    p_out,
     c_buf,
     f1_buf,
     f0_buf,
@@ -84,6 +84,7 @@
     a_t,
     q_aug,
     k_all,
+    acc,
     local_sem,
     t_send,
     t_recv,
@@ -97,6 +98,12 @@
     c_recv,
     w_send,
     w_recv,
+    nb_send,
+    nb_recv,
+    nc_send,
+    nc_recv,
+    r_send,
+    r_recv,
 ):
     me = lax.axis_index("rows")
     m, block = c_buf.shape
@@ -104,11 +111,24 @@
     step = m // CHUNKS
     tile = 512 if width % 512 == 0 else width
     tiles = width // tile
+    column = lax.axis_index("cols")
+    core = lax.rem(column, 2)
+    partner = column + 1 - 2 * core
 
     def load(src, dst, at):
         copy = pltpu.make_async_copy(src, dst, local_sem.at[at])
         copy.start()
         return copy
+
+    def near(src, dst, send, recv):
+        return pltpu.make_async_remote_copy(
+            src_ref=src,
+            dst_ref=dst,
+            send_sem=send,
+            recv_sem=recv,
+            device_id={"cols": partner},
+            device_id_type=pl.DeviceIdType.MESH,
+        )
 
     def remote(src, dst, send, recv, peer):
         return pltpu.make_async_remote_copy(
@@ -123,7 +143,7 @@
     in_c = load(c_hbm, c_buf, 0)
     in_f1 = load(f_hbm.at[:, pl.ds(block, block)], f1_buf, 1)
     in_t = load(t_hbm, t_all.at[me], 2)
-    in_q = load(q_hbm.at[:, pl.ds(pl.multiple_of(me * width, 128), width)], q_buf, 3)
+    in_q = load(q_hbm.at[:, pl.ds(pl.multiple_of((2 * me + core) * width, 128), width)], q_buf, 3)
     in_f0 = load(f_hbm.at[:, pl.ds(0, block)], f0_buf, 4)
     in_b = load(b_hbm, b_buf, 5)
 
@@ -135,7 +155,10 @@
             device_id={"rows": lax.rem(me + k, rows)},
             device_id_type=pl.DeviceIdType.MESH,
         )
-    pl.semaphore_wait(barrier, rows - 1)
+    pl.semaphore_signal(
+        barrier, inc=1, device_id={"cols": partner}, device_id_type=pl.DeviceIdType.MESH
+    )
+    pl.semaphore_wait(barrier, rows)
 
     def t_copy(k):
         return remote(
@@ -176,8 +199,8 @@
 
     def c_copy(k):
         return remote(
-            w_all.at[:, part(me)],
-            w_all.at[:, part(me)],
+            w_all.at[pl.ds(0, m), part(me)],
+            w_all.at[pl.ds(0, m), part(me)],
             c_send.at[k - 1],
             c_recv.at[me],
             lax.rem(me + k, rows),
@@ -192,6 +215,24 @@
             lax.rem(me + k, rows),
         )
 
+    def near_block(r):
+        return near(
+            w_all.at[pl.ds(0, m), part(r)],
+            w_all.at[pl.ds(m, m), part(r)],
+            nb_send.at[r],
+            nb_recv.at[r],
+        )
+
+    def near_chunk(r, c):
+        return near(
+            w_all.at[chunk(c), part(r)],
+            w_all.at[pl.ds(m + c * step, step), part(r)],
+            nc_send.at[r, c],
+            nc_recv.at[r, c],
+        )
+
+    others = [rows - 1] + list(range(1, rows - 1))
+
     in_c.wait()
     in_f1.wait()
 
@@ -203,7 +244,7 @@
             part1[at] = product(c_buf[at], h1_buf[...], l1_buf[...]).astype(SEND_TYPE)
             for c in range(half * CHUNKS // 2, (half + 1) * CHUNKS // 2):
                 p1_copy(c, me - 2).start()
-        w_all[:, part(me)] = c_buf[...].astype(BF16)
+        w_all[:m, part(me)] = c_buf[...].astype(BF16)
 
     in_f0.wait()
     in_b.wait()
@@ -267,11 +308,6 @@
 
     lax.fori_loop(0, 2, kernel_block, 0)
 
-    @pl.when(me >= 2)
-    def _():
-        for k in range(1, rows):
-            c_copy(k).start()
-
     @pl.when(me == 1)
     def _():
         for c in range(CHUNKS):
@@ -285,10 +321,21 @@
             tt_copy(c).start()
             w_all[chunk(c), part(1)] = value.astype(BF16)
         for c in range(CHUNKS):
-            for k in range(1, rows):
+            for k in others:
                 w_copy(c, k).start()
-
-    lax.fori_loop(2, rows, kernel_block, 0)
+            near_chunk(1, c).start()
+
+    lax.fori_loop(2, 3, kernel_block, 0)
+
+    @pl.when(me >= 2)
+    def _():
+        for c in range(CHUNKS):
+            p1_copy(c, me - 2).wait_send()
+        for k in range(1, rows):
+            c_copy(k).start()
+        near_block(me).start()
+
+    lax.fori_loop(3, rows, kernel_block, 0)
 
     @pl.when(me == 0)
     def _():
@@ -302,10 +349,11 @@
             value = product(c_buf[chunk(c)] - rest, h1_buf[...], l1_buf[...])
             w_buf[chunk(c)] = value
             w_all[chunk(c), part(0)] = value.astype(BF16)
-            for k in range(1, rows):
+            for k in others:
                 w_copy(c, k).start()
-
-    def w_wait(r):
+            near_chunk(0, c).start()
+
+    def pass_on(r):
         @pl.when(me != r)
         def _():
             for c in range(CHUNKS):
@@ -316,37 +364,78 @@
                     w_recv.at[r, c],
                     0,
                 ).wait_recv()
-
-    def later_block(r, carry):
+                near_chunk(r, c).start()
+
+        for c in range(CHUNKS):
+            near_chunk(r, c).wait_recv()
+
+    def pass_block(r, carry):
         @pl.when(r != me)
         def _():
             remote(
-                w_all.at[:, part(r)], w_all.at[:, part(r)], c_send.at[0], c_recv.at[r], 0
+                w_all.at[pl.ds(0, m), part(r)],
+                w_all.at[pl.ds(0, m), part(r)],
+                c_send.at[0],
+                c_recv.at[r],
+                0,
             ).wait_recv()
+            near_block(r).start()
 
         return carry
 
-    lax.fori_loop(2, rows, later_block, 0)
-    w_wait(1)
-
-    def first_tile(j, carry):
+    def block_arrived(r, carry):
+        near_block(r).wait_recv()
+        return carry
+
+    lax.fori_loop(2, rows, pass_block, 0)
+    lax.fori_loop(2, rows, block_arrived, 0)
+
+    def later_tile(j, carry):
         at = pl.ds(pl.multiple_of(j * tile, 128), tile)
         acc[:, at] = jnp.dot(
-            w_all[:, block:], k_all[block:, at], preferred_element_type=F32
+            w_all[:, 2 * block :], k_all[2 * block :, at], preferred_element_type=F32
         )
         return carry
 
-    lax.fori_loop(0, tiles, first_tile, 0)
-    w_wait(0)
-
-    def last_tile(j, carry):
+    lax.fori_loop(0, tiles, later_tile, 0)
+    pass_on(1)
+
+    def one_tile(j, carry):
         at = pl.ds(pl.multiple_of(j * tile, 128), tile)
         acc[:, at] += jnp.dot(
+            w_all[:, block : 2 * block], k_all[block : 2 * block, at], preferred_element_type=F32
+        )
+        return carry
+
+    lax.fori_loop(0, tiles, one_tile, 0)
+    pass_on(0)
+
+    def result_copy(j):
+        at = pl.ds(j * tile, tile)
+        out_at = pl.ds(pl.multiple_of(core * width + j * tile, 128), tile)
+        return near(acc.at[pl.ds(m, m), at], p_out.at[:, out_at], r_send.at[j], r_recv.at[j])
+
+    for j in range(tiles):
+        at = pl.ds(j * tile, tile)
+        value = acc[:, at] + jnp.dot(
             w_all[:, :block], k_all[:block, at], preferred_element_type=F32
         )
+        acc[m:, at] = value[m:]
+        result_copy(j).start()
+        p_out[:, pl.ds(pl.multiple_of(core * width + j * tile, 128), tile)] = value[:m]
+
+    for j in range(tiles):
+        result_copy(j).wait()
+
+    for r in range(2):
+        for c in range(CHUNKS):
+            near_chunk(r, c).wait_send()
+
+    def block_sent(r, carry):
+        near_block(r).wait_send()
         return carry
 
-    lax.fori_loop(0, tiles, last_tile, 0)
+    lax.fori_loop(2, rows, block_sent, 0)
 
     for k in range(1, rows):
         t_copy(k).wait_send()
@@ -354,7 +443,6 @@
     @pl.when(me >= 2)
     def _():
         for c in range(CHUNKS):
-            p1_copy(c, me - 2).wait_send()
             p0_copy(c, me - 2).wait_send()
         for k in range(1, rows):
             c_copy(k).wait_send()
@@ -377,7 +465,8 @@
     rows = lax.axis_size("rows")
     m, block = coefficients.shape
     params = train_inputs.shape[0]
-    width = query_points.shape[1] // rows
+    width = query_points.shape[1] // (2 * rows)
+    tile = 512 if width % 512 == 0 else width
     padded = -(-params // 16) * 16
     depth = -(-(6 * padded + 16) // 128) * 128
     anywhere = pl.BlockSpec(memory_space=pltpu.HBM)
@@ -387,7 +476,7 @@
         functools.partial(kernel, rows),
         out_shape=(
             pltpu.VMEM((m, block), F32),
-            pltpu.VMEM((m, width), F32),
+            pltpu.VMEM((m, 2 * width), F32),
         ),
         in_specs=[pl.BlockSpec(memory_space=pltpu.SMEM)] + [anywhere] * 5,
         out_specs=(pl.BlockSpec(memory_space=pltpu.VMEM),) * 2,
@@ -407,10 +496,11 @@
             vmem((rows - 2, m, block), SEND_TYPE),
             vmem((rows - 2, m, block), SEND_TYPE),
             vmem((m, block), SEND_TYPE),
-            vmem((m, rows * block), BF16),
+            vmem((2 * m, rows * block), BF16),
             vmem((block, depth), BF16),
             vmem((depth, width), BF16),
             vmem((rows * block, width), BF16),
+            vmem((2 * m, width), F32),
             dma((6,)),
             dma((rows - 1,)),
             dma((rows,)),
@@ -424,6 +514,12 @@
             dma((rows,)),
             dma((CHUNKS, rows - 1)),
             dma((2, CHUNKS)),
+            dma((rows,)),
+            dma((rows,)),
+            dma((2, CHUNKS)),
+            dma((2, CHUNKS)),
+            dma((width // tile,)),
+            dma((width // tile,)),
         ],
         compiler_params=pltpu.CompilerParams(
             collective_id=0, has_side_effects=True, vmem_limit_bytes=60 * 1024 * 1024

time: 28.4 us -> 29.5 us (1.039)
  Pallas kernels: 25.7 us -> 26.5 us
    pallas_call x1, Pallas kernels: 25.7 us -> 26.5 us  [on_device(): pl.pallas_call(functools.partial(kernel, rows), out_shape=(pltpu.VMEM((m,...]
where the time goes in v5:
time: 29.5 us; the launch traced here: 29 us
  Pallas kernels  26.5 us (90%)
  other arithmetic  1.85 us (6%)
  between operations  0.67 us (2%)
    pallas_call x1, Pallas kernels, on_device(): pl.pallas_call(functools.partial(kernel, rows), out_shape=(pltpu.VMEM((m,...  26.5 us
    mul x1, other arithmetic, on_device(): return (weights, summed * amplitude[:, None])  1.11 us
    select_n x1, other arithmetic, on_device(): weights = jnp.where(lax.axis_index('rows') < 2, solved, coefficients)  0.74 us

profile of v5, /device:TPU:0, one launch (start us, length us, event | category | flops | bytes accessed | tf_op | source)
XLA Modules:
  0.0 29.0 jit_solution(3867663318784435863)
XLA Ops:
  0.6 0.0 copy-start
  0.6 0.0 copy-start.1
  0.7 26.5 %shard_map.86 = (f32[128,512]{1,0:T(8,128)S(1)}, f32[128,2048]{1,0:T(8,128)S(1)}) custom-call(f32[14]{0:T(128)} %inv_ref.1, f32[128,512]{1,0:T(8,128)} %c_hbm.1, f32[512,1024]{1,0:T(8,128)} %f_hbm.1, f32[512,512]{1,0:T(8,128)} %b_hbm.1, f32[14,512]{1,0:T(8,128)} %t_hbm.1, f32[14,8192]{1,0:T(8,128)} %q_hbm.1), custom_call_target="tpu_custom_call" | custom-call | tf_op jit(solution)/shard_map/pallas_call | solution.py:475
  27.2 0.0 copy-done
  27.2 0.7 %broadcast_select_fusion = f32[128,512]{1,0:T(8,128)} fusion(f32[128,512]{1,0:T(8,128)S(1)} %get-tuple-element.4, f32[128,512]{1,0:T(8,128)S(1)} %copy-done, pred[]{:T(512)S(6)} %lt.3), kind=kLoop, calls=%fused_computation.1 | loop fusion | flops 65536 | bytes 786433 | tf_op jit(solution)/shard_map/jit(_where)/select_n | solution.py:528
  27.9 0.0 copy-done.1
  27.9 1.1 %broadcast_multiply_fusion = f32[128,2048]{1,0:T(8,128)} fusion(f32[128,2048]{1,0:T(8,128)S(1)} %get-tuple-element.5, f32[128]{0:T(128)S(1)} %copy-done.1), kind=kLoop, calls=%fused_computation | loop fusion | flops 262144 | bytes 2097664 | tf_op jit(solution)/shard_map/mul | solution.py:529
Async XLA Ops:
  0.6 26.5 %copy-start = (f32[128,512]{1,0:T(8,128)S(1)}, f32[128,512]{1,0:T(8,128)}, u32[]{:S(2)}) copy-start(f32[128,512]{1,0:T(8,128)} %c_hbm.1) | copy-start | bytes 786436
  0.6 27.3 %copy-start.1 = (f32[128]{0:T(128)S(1)}, f32[128]{0:T(128)}, u32[]{:S(2)}) copy-start(f32[128]{0:T(128)} %param.13) | copy-start | bytes 1540

commit v6 on v4

--- a/solution.py
+++ b/solution.py
@@ -97,6 +97,9 @@
     c_recv,
     w_send,
     w_recv,
+    relay_send,
+    k_send,
+    k_recv,
 ):
     me = lax.axis_index("rows")
     m, block = c_buf.shape
@@ -104,6 +107,10 @@
     step = m // CHUNKS
     tile = 512 if width % 512 == 0 else width
     tiles = width // tile
+    column = lax.axis_index("cols")
+    core = lax.rem(column, 2)
+    partner = column + 1 - 2 * core
+    relayed = rows == 4
 
     def load(src, dst, at):
         copy = pltpu.make_async_copy(src, dst, local_sem.at[at])
@@ -123,7 +130,7 @@
     in_c = load(c_hbm, c_buf, 0)
     in_f1 = load(f_hbm.at[:, pl.ds(block, block)], f1_buf, 1)
     in_t = load(t_hbm, t_all.at[me], 2)
-    in_q = load(q_hbm.at[:, pl.ds(pl.multiple_of(me * width, 128), width)], q_buf, 3)
+    in_q = load(q_hbm.at[:, pl.ds(pl.multiple_of((2 * me + core) * width, 128), width)], q_buf, 3)
     in_f0 = load(f_hbm.at[:, pl.ds(0, block)], f0_buf, 4)
     in_b = load(b_hbm, b_buf, 5)
 
@@ -135,7 +142,10 @@
             device_id={"rows": lax.rem(me + k, rows)},
             device_id_type=pl.DeviceIdType.MESH,
         )
-    pl.semaphore_wait(barrier, rows - 1)
+    pl.semaphore_signal(
+        barrier, inc=1, device_id={"cols": partner}, device_id_type=pl.DeviceIdType.MESH
+    )
+    pl.semaphore_wait(barrier, rows)
 
     def t_copy(k):
         return remote(
@@ -191,6 +201,29 @@
             w_recv.at[me, c],
             lax.rem(me + k, rows),
         )
+
+    def k_copy(r, j, half):
+        at = pl.ds(pl.multiple_of(half * width + j * tile, 128), tile)
+        return pltpu.make_async_remote_copy(
+            src_ref=k_all.at[part(r), at],
+            dst_ref=k_all.at[part(r), at],
+            send_sem=k_send.at[r, j],
+            recv_sem=k_recv.at[r, j],
+            device_id={"cols": partner},
+            device_id_type=pl.DeviceIdType.MESH,
+        )
+
+    def relay_copy(c, r, to):
+        return remote(
+            w_all.at[chunk(c), part(r)],
+            w_all.at[chunk(c), part(r)],
+            relay_send.at[c],
+            w_recv.at[r, c],
+            to,
+        )
+
+    from_one = [3, 2] if relayed else [rows - 1] + list(range(1, rows - 1))
+    from_zero = [2, 1] if relayed else list(range(1, rows))
 
     in_c.wait()
     in_f1.wait()
@@ -249,28 +282,22 @@
             parts.append(jnp.zeros((depth - used, block), F32))
         a_t[...] = jnp.concatenate(parts, axis=0).T.astype(BF16)
 
-    def kernel_tile(j):
-        at = pl.ds(pl.multiple_of(j * tile, 128), tile)
-        y = jnp.dot(a_t[...], q_aug[:, at], preferred_element_type=F32)
-        y = jnp.maximum(y, EPSILON)
-        return at, jnp.exp(-(y * lax.rsqrt(y))).astype(BF16)
-
-    def kernel_block(r, carry):
+    def kernel_block(n, carry):
+        r = lax.rem(n + 2, rows)
         train_side(r)
 
         def store_tile(j, inner):
-            at, values = kernel_tile(j)
-            k_all[part(r), at] = values
+            here = pl.ds(pl.multiple_of(j * tile, 128), tile)
+            at = pl.ds(pl.multiple_of(core * width + j * tile, 128), tile)
+            y = jnp.dot(a_t[...], q_aug[:, here], preferred_element_type=F32)
+            y = jnp.maximum(y, EPSILON)
+            k_all[part(r), at] = jnp.exp(-(y * lax.rsqrt(y))).astype(BF16)
+            k_copy(r, j, core).start()
             return inner
 
         return lax.fori_loop(0, tiles, store_tile, carry)
 
     lax.fori_loop(0, 2, kernel_block, 0)
-
-    @pl.when(me >= 2)
-    def _():
-        for k in range(1, rows):
-            c_copy(k).start()
 
     @pl.when(me == 1)
     def _():
@@ -285,10 +312,19 @@
             tt_copy(c).start()
             w_all[chunk(c), part(1)] = value.astype(BF16)
         for c in range(CHUNKS):
-            for k in range(1, rows):
+            for k in from_one:
                 w_copy(c, k).start()
 
-    lax.fori_loop(2, rows, kernel_block, 0)
+    lax.fori_loop(2, 3, kernel_block, 0)
+
+    @pl.when(me >= 2)
+    def _():
+        for c in range(CHUNKS):
+            p1_copy(c, me - 2).wait_send()
+        for k in range(1, rows):
+            c_copy(k).start()
+
+    lax.fori_loop(3, rows, kernel_block, 0)
 
     @pl.when(me == 0)
     def _():
@@ -302,20 +338,37 @@
             value = product(c_buf[chunk(c)] - rest, h1_buf[...], l1_buf[...])
             w_buf[chunk(c)] = value
             w_all[chunk(c), part(0)] = value.astype(BF16)
-            for k in range(1, rows):
+            for k in from_zero:
                 w_copy(c, k).start()
 
     def w_wait(r):
         @pl.when(me != r)
         def _():
             for c in range(CHUNKS):
-                remote(
-                    w_all.at[chunk(c), part(r)],
-                    w_all.at[chunk(c), part(r)],
-                    w_send.at[c, 0],
-                    w_recv.at[r, c],
-                    0,
-                ).wait_recv()
+                relay_copy(c, r, 0).wait_recv()
+                if relayed:
+
+                    @pl.when(me == 2 + r)
+                    def _():
+                        relay_copy(c, r, 3 - r).start()
+
+    def k_wait(r, carry):
+        for j in range(tiles):
+            k_copy(r, j, 1 - core).wait_recv()
+        return carry
+
+    def add_blocks(first, last, fresh):
+        def add_tile(j, carry):
+            at = pl.ds(pl.multiple_of(j * tile, 128), tile)
+            value = jnp.dot(
+                w_all[:, first * block : last * block],
+                k_all[first * block : last * block, at],
+                preferred_element_type=F32,
+            )
+            acc[:, at] = value if fresh else acc[:, at] + value
+            return carry
+
+        lax.fori_loop(0, 2 * tiles, add_tile, 0)
 
     def later_block(r, carry):
         @pl.when(r != me)
@@ -324,29 +377,23 @@
                 w_all.at[:, part(r)], w_all.at[:, part(r)], c_send.at[0], c_recv.at[r], 0
             ).wait_recv()
 
+        return k_wait(r, carry)
+
+    lax.fori_loop(2, rows, later_block, 0)
+    add_blocks(2, rows, True)
+    w_wait(1)
+    k_wait(1, 0)
+    add_blocks(1, 2, False)
+    k_wait(0, 0)
+    w_wait(0)
+    add_blocks(0, 1, False)
+
+    def k_sent(r, carry):
+        for j in range(tiles):
+            k_copy(r, j, core).wait_send()
         return carry
 
-    lax.fori_loop(2, rows, later_block, 0)
-    w_wait(1)
-
-    def first_tile(j, carry):
-        at = pl.ds(pl.multiple_of(j * tile, 128), tile)
-        acc[:, at] = jnp.dot(
-            w_all[:, block:], k_all[block:, at], preferred_element_type=F32
-        )
-        return carry
-
-    lax.fori_loop(0, tiles, first_tile, 0)
-    w_wait(0)
-
-    def last_tile(j, carry):
-        at = pl.ds(pl.multiple_of(j * tile, 128), tile)
-        acc[:, at] += jnp.dot(
-            w_all[:, :block], k_all[:block, at], preferred_element_type=F32
-        )
-        return carry
-
-    lax.fori_loop(0, tiles, last_tile, 0)
+    lax.fori_loop(0, rows, k_sent, 0)
 
     for k in range(1, rows):
         t_copy(k).wait_send()
@@ -354,8 +401,9 @@
     @pl.when(me >= 2)
     def _():
         for c in range(CHUNKS):
-            p1_copy(c, me - 2).wait_send()
             p0_copy(c, me - 2).wait_send()
+            if relayed:
+                relay_copy(c, 0, 0).wait_send()
         for k in range(1, rows):
             c_copy(k).wait_send()
 
@@ -364,11 +412,13 @@
         for c in range(CHUNKS):
             tt_copy(c).wait_send()
 
-    @pl.when(me < 2)
-    def _():
-        for c in range(CHUNKS):
-            for k in range(1, rows):
-                w_copy(c, k).wait_send()
+    for r, peers in ((0, from_zero), (1, from_one)):
+
+        @pl.when(me == r)
+        def _():
+            for c in range(CHUNKS):
+                for k in peers:
+                    w_copy(c, k).wait_send()
 
 
 def on_device(
@@ -377,7 +427,8 @@
     rows = lax.axis_size("rows")
     m, block = coefficients.shape
     params = train_inputs.shape[0]
-    width = query_points.shape[1] // rows
+    width = query_points.shape[1] // (2 * rows)
+    tile = 512 if width % 512 == 0 else width
     padded = -(-params // 16) * 16
     depth = -(-(6 * padded + 16) // 128) * 128
     anywhere = pl.BlockSpec(memory_space=pltpu.HBM)
@@ -387,7 +438,7 @@
         functools.partial(kernel, rows),
         out_shape=(
             pltpu.VMEM((m, block), F32),
-            pltpu.VMEM((m, width), F32),
+            pltpu.VMEM((m, 2 * width), F32),
         ),
         in_specs=[pl.BlockSpec(memory_space=pltpu.SMEM)] + [anywhere] * 5,
         out_specs=(pl.BlockSpec(memory_space=pltpu.VMEM),) * 2,
@@ -410,7 +461,7 @@
             vmem((m, rows * block), BF16),
             vmem((block, depth), BF16),
             vmem((depth, width), BF16),
-            vmem((rows * block, width), BF16),
+            vmem((rows * block, 2 * width), BF16),
             dma((6,)),
             dma((rows - 1,)),
             dma((rows,)),
@@ -424,6 +475,9 @@
             dma((rows,)),
             dma((CHUNKS, rows - 1)),
             dma((2, CHUNKS)),
+            dma((CHUNKS,)),
+            dma((rows, width // tile)),
+            dma((rows, width // tile)),
         ],
         compiler_params=pltpu.CompilerParams(
             collective_id=0, has_side_effects=True, vmem_limit_bytes=60 * 1024 * 1024

time: 28.4 us -> 29.4 us (1.035)
  the two profiles are of different devices: /device:TPU:0 before, /device:TPU:14 now
where the time goes in v6:
time: 29.4 us; the launch traced here: 29.2 us
  Pallas kernels  26.7 us (91%)
  other arithmetic  1.85 us (6%)
  between operations  0.67 us (2%)
    pallas_call x1, Pallas kernels, on_device(): pl.pallas_call(functools.partial(kernel, rows), out_shape=(pltpu.VMEM((m,...  26.7 us
    mul x1, other arithmetic, on_device(): return (weights, summed * amplitude[:, None])  1.11 us
    select_n x1, other arithmetic, on_device(): weights = jnp.where(lax.axis_index('rows') < 2, solved, coefficients)  0.74 us

profile of v6, /device:TPU:14, one launch (start us, length us, event | category | flops | bytes accessed | tf_op | source)
XLA Modules:
  0.0 29.2 jit_solution(11161642722498582998)
XLA Ops:
  0.6 0.0 copy-start
  0.6 0.0 copy-start.1
  0.7 26.7 %shard_map.86 = (f32[128,512]{1,0:T(8,128)S(1)}, f32[128,2048]{1,0:T(8,128)S(1)}) custom-call(f32[14]{0:T(128)} %inv_ref.1, f32[128,512]{1,0:T(8,128)} %c_hbm.1, f32[512,1024]{1,0:T(8,128)} %f_hbm.1, f32[512,512]{1,0:T(8,128)} %b_hbm.1, f32[14,512]{1,0:T(8,128)} %t_hbm.1, f32[14,8192]{1,0:T(8,128)} %q_hbm.1), custom_call_target="tpu_custom_call" | custom-call | tf_op jit(solution)/shard_map/pallas_call | solution.py:437
  27.4 0.0 copy-done
  27.4 0.7 %broadcast_select_fusion = f32[128,512]{1,0:T(8,128)} fusion(f32[128,512]{1,0:T(8,128)S(1)} %get-tuple-element.4, f32[128,512]{1,0:T(8,128)S(1)} %copy-done, pred[]{:T(512)S(6)} %lt.3), kind=kLoop, calls=%fused_computation.1 | loop fusion | flops 65536 | bytes 786433 | tf_op jit(solution)/shard_map/jit(_where)/select_n | solution.py:486
  28.1 0.0 copy-done.1
  28.1 1.1 %broadcast_multiply_fusion = f32[128,2048]{1,0:T(8,128)} fusion(f32[128,2048]{1,0:T(8,128)S(1)} %get-tuple-element.5, f32[128]{0:T(128)S(1)} %copy-done.1), kind=kLoop, calls=%fused_computation | loop fusion | flops 262144 | bytes 2097664 | tf_op jit(solution)/shard_map/mul | solution.py:487
Async XLA Ops:
  0.6 26.7 %copy-start = (f32[128,512]{1,0:T(8,128)S(1)}, f32[128,512]{1,0:T(8,128)}, u32[]{:S(2)}) copy-start(f32[128,512]{1,0:T(8,128)} %c_hbm.1) | copy-start | bytes 786436
  0.6 27.5 %copy-start.1 = (f32[128]{0:T(128)S(1)}, f32[128]{0:T(128)}, u32[]{:S(2)}) copy-start(f32[128]{0:T(128)} %param.13) | copy-start | bytes 1540

commit v7 on v6

--- a/solution.py
+++ b/solution.py
@@ -97,7 +97,6 @@
     c_recv,
     w_send,
     w_recv,
-    relay_send,
     k_send,
     k_recv,
 ):
@@ -110,7 +109,6 @@
     column = lax.axis_index("cols")
     core = lax.rem(column, 2)
     partner = column + 1 - 2 * core
-    relayed = rows == 4
 
     def load(src, dst, at):
         copy = pltpu.make_async_copy(src, dst, local_sem.at[at])
@@ -213,17 +211,8 @@
             device_id_type=pl.DeviceIdType.MESH,
         )
 
-    def relay_copy(c, r, to):
-        return remote(
-            w_all.at[chunk(c), part(r)],
-            w_all.at[chunk(c), part(r)],
-            relay_send.at[c],
-            w_recv.at[r, c],
-            to,
-        )
-
-    from_one = [3, 2] if relayed else [rows - 1] + list(range(1, rows - 1))
-    from_zero = [2, 1] if relayed else list(range(1, rows))
+    from_one = [rows - 1] + list(range(1, rows - 1))
+    from_zero = list(range(rows - 1, 0, -1))
 
     in_c.wait()
     in_f1.wait()
@@ -345,12 +334,13 @@
         @pl.when(me != r)
         def _():
             for c in range(CHUNKS):
-                relay_copy(c, r, 0).wait_recv()
-                if relayed:
-
-                    @pl.when(me == 2 + r)
-                    def _():
-                        relay_copy(c, r, 3 - r).start()
+                remote(
+                    w_all.at[chunk(c), part(r)],
+                    w_all.at[chunk(c), part(r)],
+                    w_send.at[c, 0],
+                    w_recv.at[r, c],
+                    0,
+                ).wait_recv()
 
     def k_wait(r, carry):
         for j in range(tiles):
@@ -402,8 +392,6 @@
     def _():
         for c in range(CHUNKS):
             p0_copy(c, me - 2).wait_send()
-            if relayed:
-                relay_copy(c, 0, 0).wait_send()
         for k in range(1, rows):
             c_copy(k).wait_send()
 
@@ -475,7 +463,6 @@
             dma((rows,)),
             dma((CHUNKS, rows - 1)),
             dma((2, CHUNKS)),
-            dma((CHUNKS,)),
             dma((rows, width // tile)),
             dma((rows, width // tile)),
         ],

time: 29.4 us -> 28.1 us (0.956)
  the two profiles are of different devices: /device:TPU:14 before, /device:TPU:0 now
where the time goes in v7:
time: 28.1 us; the launch traced here: 27.9 us
  Pallas kernels  25.4 us (90%)
  other arithmetic  1.85 us (7%)
  between operations  0.67 us (2%)
    pallas_call x1, Pallas kernels, on_device(): pl.pallas_call(functools.partial(kernel, rows), out_shape=(pltpu.VMEM((m,...  25.4 us
    mul x1, other arithmetic, on_device(): return (weights, summed * amplitude[:, None])  1.11 us
    select_n x1, other arithmetic, on_device(): weights = jnp.where(lax.axis_index('rows') < 2, solved, coefficients)  0.74 us

profile of v7, /device:TPU:0, one launch (start us, length us, event | category | flops | bytes accessed | tf_op | source)
XLA Modules:
  0.0 27.9 jit_solution(10447786608092802852)
XLA Ops:
  0.6 0.0 copy-start
  0.6 0.0 copy-start.1
  0.7 25.4 %shard_map.86 = (f32[128,512]{1,0:T(8,128)S(1)}, f32[128,2048]{1,0:T(8,128)S(1)}) custom-call(f32[14]{0:T(128)} %inv_ref.1, f32[128,512]{1,0:T(8,128)} %c_hbm.1, f32[512,1024]{1,0:T(8,128)} %f_hbm.1, f32[512,512]{1,0:T(8,128)} %b_hbm.1, f32[14,512]{1,0:T(8,128)} %t_hbm.1, f32[14,8192]{1,0:T(8,128)} %q_hbm.1), custom_call_target="tpu_custom_call" | custom-call | tf_op jit(solution)/shard_map/pallas_call | solution.py:425
  26.0 0.0 copy-done
  26.1 0.7 %broadcast_select_fusion = f32[128,512]{1,0:T(8,128)} fusion(f32[128,512]{1,0:T(8,128)S(1)} %get-tuple-element.4, f32[128,512]{1,0:T(8,128)S(1)} %copy-done, pred[]{:T(512)S(6)} %lt.3), kind=kLoop, calls=%fused_computation.1 | loop fusion | flops 65536 | bytes 786433 | tf_op jit(solution)/shard_map/jit(_where)/select_n | solution.py:473
  26.8 0.0 copy-done.1
  26.8 1.1 %broadcast_multiply_fusion = f32[128,2048]{1,0:T(8,128)} fusion(f32[128,2048]{1,0:T(8,128)S(1)} %get-tuple-element.5, f32[128]{0:T(128)S(1)} %copy-done.1), kind=kLoop, calls=%fused_computation | loop fusion | flops 262144 | bytes 2097664 | tf_op jit(solution)/shard_map/mul | solution.py:474
Async XLA Ops:
  0.6 25.4 %copy-start = (f32[128,512]{1,0:T(8,128)S(1)}, f32[128,512]{1,0:T(8,128)}, u32[]{:S(2)}) copy-start(f32[128,512]{1,0:T(8,128)} %c_hbm.1) | copy-start | bytes 786436
  0.6 26.2 %copy-start.1 = (f32[128]{0:T(128)S(1)}, f32[128]{0:T(128)}, u32[]{:S(2)}) copy-start(f32[128]{0:T(128)} %param.13) | copy-start | bytes 1540

commit v8 on v7

--- a/solution.py
+++ b/solution.py
@@ -97,6 +97,7 @@
     c_recv,
     w_send,
     w_recv,
+    relay_send,
     k_send,
     k_recv,
 ):
@@ -211,7 +212,8 @@
             device_id_type=pl.DeviceIdType.MESH,
         )
 
-    from_one = [rows - 1] + list(range(1, rows - 1))
+    relayed = rows == 4
+    from_one = [rows - 1, 2] if relayed else [rows - 1] + list(range(1, rows - 1))
     from_zero = list(range(rows - 1, 0, -1))
 
     in_c.wait()
@@ -330,17 +332,28 @@
             for k in from_zero:
                 w_copy(c, k).start()
 
+    def w_arrival(c, r):
+        return remote(
+            w_all.at[chunk(c), part(r)],
+            w_all.at[chunk(c), part(r)],
+            relay_send.at[c],
+            w_recv.at[r, c],
+            2,
+        )
+
+    if relayed:
+
+        @pl.when(me == 3)
+        def _():
+            for c in range(CHUNKS):
+                w_arrival(c, 1).wait_recv()
+                w_arrival(c, 1).start()
+
     def w_wait(r):
-        @pl.when(me != r)
+        @pl.when((me != 1) & (me != 3) if relayed and r == 1 else me != r)
         def _():
             for c in range(CHUNKS):
-                remote(
-                    w_all.at[chunk(c), part(r)],
-                    w_all.at[chunk(c), part(r)],
-                    w_send.at[c, 0],
-                    w_recv.at[r, c],
-                    0,
-                ).wait_recv()
+                w_arrival(c, r).wait_recv()
 
     def k_wait(r, carry):
         for j in range(tiles):
@@ -399,6 +412,13 @@
     def _():
         for c in range(CHUNKS):
             tt_copy(c).wait_send()
+
+    if relayed:
+
+        @pl.when(me == 3)
+        def _():
+            for c in range(CHUNKS):
+                w_arrival(c, 1).wait_send()
 
     for r, peers in ((0, from_zero), (1, from_one)):
 
@@ -463,6 +483,7 @@
             dma((rows,)),
             dma((CHUNKS, rows - 1)),
             dma((2, CHUNKS)),
+            dma((CHUNKS,)),
             dma((rows, width // tile)),
             dma((rows, width // tile)),
         ],

time: 28.1 us -> 28 us (level)
  the two profiles are of different devices: /device:TPU:0 before, /device:TPU:28 now
where the time goes in v8:
time: 28 us; the launch traced here: 27.9 us
  Pallas kernels  25.3 us (90%)
  other arithmetic  1.85 us (7%)
  between operations  0.67 us (2%)
    pallas_call x1, Pallas kernels, on_device(): pl.pallas_call(functools.partial(kernel, rows), out_shape=(pltpu.VMEM((m,...  25.3 us
    mul x1, other arithmetic, on_device(): return (weights, summed * amplitude[:, None])  1.11 us
    select_n x1, other arithmetic, on_device(): weights = jnp.where(lax.axis_index('rows') < 2, solved, coefficients)  0.74 us

profile of v8, /device:TPU:28, one launch (start us, length us, event | category | flops | bytes accessed | tf_op | source)
XLA Modules:
  0.0 27.9 jit_solution(15066890937261474066)
XLA Ops:
  0.6 0.0 copy-start
  0.6 0.0 copy-start.1
  0.7 25.3 %shard_map.86 = (f32[128,512]{1,0:T(8,128)S(1)}, f32[128,2048]{1,0:T(8,128)S(1)}) custom-call(f32[14]{0:T(128)} %inv_ref.1, f32[128,512]{1,0:T(8,128)} %c_hbm.1, f32[512,1024]{1,0:T(8,128)} %f_hbm.1, f32[512,512]{1,0:T(8,128)} %b_hbm.1, f32[14,512]{1,0:T(8,128)} %t_hbm.1, f32[14,8192]{1,0:T(8,128)} %q_hbm.1), custom_call_target="tpu_custom_call" | custom-call | tf_op jit(solution)/shard_map/pallas_call | solution.py:445
  26.0 0.0 copy-done
  26.0 0.7 %broadcast_select_fusion = f32[128,512]{1,0:T(8,128)} fusion(f32[128,512]{1,0:T(8,128)S(1)} %get-tuple-element.4, f32[128,512]{1,0:T(8,128)S(1)} %copy-done, pred[]{:T(512)S(6)} %lt.3), kind=kLoop, calls=%fused_computation.1 | loop fusion | flops 65536 | bytes 786433 | tf_op jit(solution)/shard_map/jit(_where)/select_n | solution.py:494
  26.8 0.0 copy-done.1
  26.8 1.1 %broadcast_multiply_fusion = f32[128,2048]{1,0:T(8,128)} fusion(f32[128,2048]{1,0:T(8,128)S(1)} %get-tuple-element.5, f32[128]{0:T(128)S(1)} %copy-done.1), kind=kLoop, calls=%fused_computation | loop fusion | flops 262144 | bytes 2097664 | tf_op jit(solution)/shard_map/mul | solution.py:495
Async XLA Ops:
  0.6 25.4 %copy-start = (f32[128,512]{1,0:T(8,128)S(1)}, f32[128,512]{1,0:T(8,128)}, u32[]{:S(2)}) copy-start(f32[128,512]{1,0:T(8,128)} %c_hbm.1) | copy-start | bytes 786436
  0.6 26.1 %copy-start.1 = (f32[128]{0:T(128)S(1)}, f32[128]{0:T(128)}, u32[]{:S(2)}) copy-start(f32[128]{0:T(128)} %param.13) | copy-start | bytes 1540

commit v9 on v7

--- a/solution.py
+++ b/solution.py
@@ -288,6 +288,11 @@
 
     lax.fori_loop(0, 2, kernel_block, 0)
 
+    @pl.when(me >= 2)
+    def _():
+        for k in range(1, rows):
+            c_copy(k).start()
+
     @pl.when(me == 1)
     def _():
         for c in range(CHUNKS):
@@ -300,20 +305,11 @@
             part0[chunk(c)] = product(value, h2_buf[...], l2_buf[...]).astype(SEND_TYPE)
             tt_copy(c).start()
             w_all[chunk(c), part(1)] = value.astype(BF16)
-        for c in range(CHUNKS):
-            for k in from_one:
+        for k in from_one:
+            for c in range(CHUNKS):
                 w_copy(c, k).start()
 
-    lax.fori_loop(2, 3, kernel_block, 0)
-
-    @pl.when(me >= 2)
-    def _():
-        for c in range(CHUNKS):
-            p1_copy(c, me - 2).wait_send()
-        for k in range(1, rows):
-            c_copy(k).start()
-
-    lax.fori_loop(3, rows, kernel_block, 0)
+    lax.fori_loop(2, rows, kernel_block, 0)
 
     @pl.when(me == 0)
     def _():
@@ -391,6 +387,7 @@
     @pl.when(me >= 2)
     def _():
         for c in range(CHUNKS):
+            p1_copy(c, me - 2).wait_send()
             p0_copy(c, me - 2).wait_send()
         for k in range(1, rows):
             c_copy(k).wait_send()

time: 28.1 us -> 26.9 us (0.957)
  Pallas kernels: 25.4 us -> 24.2 us
    pallas_call x1, Pallas kernels: 25.4 us -> 24.2 us  [on_device(): pl.pallas_call(functools.partial(kernel, rows), out_shape=(pltpu.VMEM((m,...]
where the time goes in v9:
time: 26.9 us; the launch traced here: 26.8 us
  Pallas kernels  24.2 us (90%)
  other arithmetic  1.85 us (7%)
  between operations  0.67 us (2%)
    pallas_call x1, Pallas kernels, on_device(): pl.pallas_call(functools.partial(kernel, rows), out_shape=(pltpu.VMEM((m,...  24.2 us
    mul x1, other arithmetic, on_device(): return (weights, summed * amplitude[:, None])  1.11 us
    select_n x1, other arithmetic, on_device(): weights = jnp.where(lax.axis_index('rows') < 2, solved, coefficients)  0.74 us

profile of v9, /device:TPU:0, one launch (start us, length us, event | category | flops | bytes accessed | tf_op | source)
XLA Modules:
  0.0 26.8 jit_solution(5402826103344668904)
XLA Ops:
  0.6 0.0 copy-start
  0.6 0.0 copy-start.1
  0.7 24.2 %shard_map.86 = (f32[128,512]{1,0:T(8,128)S(1)}, f32[128,2048]{1,0:T(8,128)S(1)}) custom-call(f32[14]{0:T(128)} %inv_ref.1, f32[128,512]{1,0:T(8,128)} %c_hbm.1, f32[512,1024]{1,0:T(8,128)} %f_hbm.1, f32[512,512]{1,0:T(8,128)} %b_hbm.1, f32[14,512]{1,0:T(8,128)} %t_hbm.1, f32[14,8192]{1,0:T(8,128)} %q_hbm.1), custom_call_target="tpu_custom_call" | custom-call | tf_op jit(solution)/shard_map/pallas_call | solution.py:422
  24.9 0.0 copy-done
  24.9 0.7 %broadcast_select_fusion = f32[128,512]{1,0:T(8,128)} fusion(f32[128,512]{1,0:T(8,128)S(1)} %get-tuple-element.4, f32[128,512]{1,0:T(8,128)S(1)} %copy-done, pred[]{:T(512)S(6)} %lt.3), kind=kLoop, calls=%fused_computation.1 | loop fusion | flops 65536 | bytes 786433 | tf_op jit(solution)/shard_map/jit(_where)/select_n | solution.py:470
  25.7 0.0 copy-done.1
  25.7 1.1 %broadcast_multiply_fusion = f32[128,2048]{1,0:T(8,128)} fusion(f32[128,2048]{1,0:T(8,128)S(1)} %get-tuple-element.5, f32[128]{0:T(128)S(1)} %copy-done.1), kind=kLoop, calls=%fused_computation | loop fusion | flops 262144 | bytes 2097664 | tf_op jit(solution)/shard_map/mul | solution.py:471
Async XLA Ops:
  0.6 24.3 %copy-start = (f32[128,512]{1,0:T(8,128)S(1)}, f32[128,512]{1,0:T(8,128)}, u32[]{:S(2)}) copy-start(f32[128,512]{1,0:T(8,128)} %c_hbm.1) | copy-start | bytes 786436
  0.6 25.0 %copy-start.1 = (f32[128]{0:T(128)S(1)}, f32[128]{0:T(128)}, u32[]{:S(2)}) copy-start(f32[128]{0:T(128)} %param.13) | copy-start | bytes 1540
